TPU v7x, 128 devices: a whole 4x4x4 slice. The times are simulated.
128 devices in a mesh: row: 8 (over z, core), col: 16 (over x, y).
Axes of the slice: x: 4, y: 4, z: 4, core: 2. Of those that a mesh axis runs over, the one named last changes fastest.
Arguments:
- rhs: float32 [128, 128, 384], P('row', 'col'), may hold values from -10 to 10
- storage: float32 [128, 128, 384], P('row', 'col'), may hold values from 0.02 to 0.5
- class_id: int32 [128, 128, 96], P('row', 'col'), may hold values from 0 to 7
- class_conductivity: float32 [8], replicated, may hold values from 0.2 to 5
- basis: bfloat16 [64, 128, 128, 384], P(None, 'row', 'col'), may hold values from -1 to 1
Outputs:
- solution: float32 [128, 128, 384], P('row', 'col')
- residual: float32 [128, 128, 384], P('row', 'col')
All inputs are finite; a program needn't handle non-finite values.
Results may differ from a plain program's by a relative error of at most 0.0091.
Values may be sent and summed in bfloat16 or wider, within the bound.
No kernel may reach another device: no remote copies, remote signals or barrier semaphores. Data moves between devices by JAX's collectives and lax.ppermute only.
A program may use at most 192 MiB of HBM per device.

v0:
```python
import jax
import jax.numpy as jnp
from jax import lax
from jax.sharding import PartitionSpec as P

ITERS = 2
SWEEPS = 4


relax = 0.8
highest = lax.Precision.HIGHEST


def extended_2(cells, sides, width):
    for axis, dim in sides:
        count = lax.axis_size(axis)
        ends = count - 1
        head = lax.slice_in_dim(cells, 0, width, axis=dim)
        tail = lax.slice_in_dim(cells, cells.shape[dim] - width, cells.shape[dim], axis=dim)
        cells = jnp.concatenate(
            [
                lax.ppermute(tail, axis, [(i, (i + 1) % count) for i in range(ends)]),
                cells,
                lax.ppermute(head, axis, [((i + 1) % count, i) for i in range(ends)]),
            ],
            axis=dim,
        )
    return cells


def harmonic(left, right):
    return 2.0 * left * right / (left + right)


def conductances(storage, class_id, class_conductivity):
    labels = jnp.arange(class_conductivity.shape[0], dtype=jnp.int32)
    tiles = jnp.sum(
        jnp.where(class_id[..., None] == labels, class_conductivity, jnp.float32(0.0)), axis=-1
    )
    tile_len = storage.shape[2] // class_id.shape[2]
    cells = jnp.repeat(tiles, tile_len, axis=2)
    lateral = extended_2(cells, (("row", 0), ("col", 1)), 1)
    vertical = jnp.pad(cells, ((0, 0), (0, 0), (1, 1)))
    faces = (
        harmonic(cells, lateral[:-2, 1:-1]),
        harmonic(cells, lateral[2:, 1:-1]),
        harmonic(cells, lateral[1:-1, :-2]),
        harmonic(cells, lateral[1:-1, 2:]),
        harmonic(cells, vertical[:, :, :-2]),
        harmonic(cells, vertical[:, :, 2:]),
    )
    diagonal = storage + faces[0] + faces[1] + faces[2] + faces[3] + faces[4] + faces[5]
    return (faces, diagonal)


def operate(field, faces, diagonal):
    lateral = extended_2(field, (("row", 0), ("col", 1)), 1)
    vertical = jnp.pad(field, ((0, 0), (0, 0), (1, 1)))
    result = diagonal * field
    result = result - faces[0] * lateral[:-2, 1:-1]
    result = result - faces[1] * lateral[2:, 1:-1]
    result = result - faces[2] * lateral[1:-1, :-2]
    result = result - faces[3] * lateral[1:-1, 2:]
    result = result - faces[4] * vertical[:, :, :-2]
    result = result - faces[5] * vertical[:, :, 2:]
    return result


def local_stencil(field, faces, diagonal):
    padded = jnp.pad(field, ((0, 0), (1, 1), (1, 1), (1, 1)))
    result = diagonal * field
    result = result - faces[0] * padded[:, :-2, 1:-1, 1:-1]
    result = result - faces[1] * padded[:, 2:, 1:-1, 1:-1]
    result = result - faces[2] * padded[:, 1:-1, :-2, 1:-1]
    result = result - faces[3] * padded[:, 1:-1, 2:, 1:-1]
    result = result - faces[4] * padded[:, 1:-1, 1:-1, :-2]
    result = result - faces[5] * padded[:, 1:-1, 1:-1, 2:]
    return result


def invert(block):
    lower = jnp.linalg.cholesky(block)
    identity = jnp.eye(block.shape[-1], dtype=jnp.float32)
    lower_inv = lax.linalg.triangular_solve(lower, identity, left_side=True, lower=True)
    return jnp.dot(lower_inv.T, lower_inv, precision=highest)


def face_block(own_face, weight, neighbour):
    basis_size = own_face.shape[0]
    scaled = (weight * own_face).astype(jnp.bfloat16).reshape(basis_size, -1)
    return -lax.dot_general(
        scaled,
        neighbour.reshape(basis_size, -1),
        (((1,), (1,)), ((), ())),
        preferred_element_type=jnp.float32,
    )


def coarse_blocks(basis, faces, diagonal):
    basis_size = basis.shape[0]
    applied = local_stencil(basis, faces, diagonal).astype(jnp.bfloat16)
    galerkin = lax.dot_general(
        basis.reshape(basis_size, -1),
        applied.reshape(basis_size, -1),
        (((1,), (1,)), ((), ())),
        preferred_element_type=jnp.float32,
    )
    block_diag = 0.5 * (galerkin + galerkin.T)
    extended = extended_2(basis, (("row", 1), ("col", 2)), 1)
    off_blocks = jnp.stack(
        [
            face_block(basis[:, 0], faces[0][0], extended[:, 0, 1:-1]),
            face_block(basis[:, -1], faces[1][-1], extended[:, -1, 1:-1]),
            face_block(basis[:, :, 0], faces[2][:, 0], extended[:, 1:-1, 0]),
            face_block(basis[:, :, -1], faces[3][:, -1], extended[:, 1:-1, -1]),
        ]
    )
    return (block_diag, off_blocks)


def coarse_local(rhs_coarse, block_diag, inverse, off_blocks):
    iterate = relax * jnp.dot(inverse, rhs_coarse, precision=highest)
    for sweep_index in range(SWEEPS - 1):
        beside_all = extended_2(iterate[None, None, :], (("row", 0), ("col", 1)), 1)
        product = jnp.dot(block_diag, iterate, precision=highest)
        product = product + jnp.dot(off_blocks[0], beside_all[0, 1], precision=highest)
        product = product + jnp.dot(off_blocks[1], beside_all[2, 1], precision=highest)
        product = product + jnp.dot(off_blocks[2], beside_all[1, 0], precision=highest)
        product = product + jnp.dot(off_blocks[3], beside_all[1, 2], precision=highest)
        iterate = iterate + relax * jnp.dot(inverse, rhs_coarse - product, precision=highest)
    return iterate


def project(basis_flat, field):
    return jnp.dot(
        basis_flat, field.astype(jnp.bfloat16).reshape(-1), preferred_element_type=jnp.float32
    )


def expand(basis_flat, coeffs, shape):
    return jnp.dot(
        coeffs.astype(jnp.bfloat16), basis_flat, preferred_element_type=jnp.float32
    ).reshape(shape)


def body(rhs, storage, class_id, class_conductivity, basis):
    faces, diagonal = conductances(storage, class_id, class_conductivity)
    block_diag, off_blocks = coarse_blocks(basis, faces, diagonal)
    inverse = invert(block_diag)
    basis_size = basis.shape[0]
    basis_flat = basis.reshape(basis_size, -1)
    shape = rhs.shape

    def solve(rhs_coarse):
        return coarse_local(rhs_coarse, block_diag, inverse, off_blocks)

    solution = expand(basis_flat, solve(project(basis_flat, rhs)), shape)
    residual = rhs - operate(solution, faces, diagonal)
    coeffs = solve(project(basis_flat, operate(residual, faces, diagonal)))
    direction = residual - expand(basis_flat, coeffs, shape)
    norm_now = lax.psum(jnp.sum(residual * residual), ("row", "col"))
    for step_index in range(ITERS):
        image = operate(direction, faces, diagonal)
        alpha = norm_now / lax.psum(jnp.sum(direction * image), ("row", "col"))
        solution = solution + alpha * direction
        residual = residual - alpha * image
        norm_next = lax.psum(jnp.sum(residual * residual), ("row", "col"))
        if step_index + 1 < ITERS:
            coeffs = solve(project(basis_flat, operate(residual, faces, diagonal)))
            direction = (
                norm_next / norm_now * direction + residual - expand(basis_flat, coeffs, shape)
            )
            norm_now = norm_next
    return (solution, residual)


def solution(mesh):
    placed = (
        P("row", "col", None),
        P("row", "col", None),
        P("row", "col", None),
        P(),
        P(None, "row", "col", None),
    )
    return jax.shard_map(
        body,
        mesh=mesh,
        in_specs=placed,
        out_specs=(P("row", "col", None), P("row", "col", None)),
        check_vma=False,
    )
```

profile of v0, /device:TPU:1, one launch (start us, length us, event | category | flops | bytes accessed | tf_op | source)
XLA Modules:
  0.0 615.0 jit_solution(13268690187890628463)
XLA Ops:
  2.0 5.0 collective-permute-start
  9.5 6.5 %copy.367 = bf16[64,16,8,384]{3,0,2,1:T(8,128)(2,1)S(1)} copy(bf16[64,16,8,384]{3,2,1,0:T(8,128)(2,1)} %param.9) | data formatting | bytes 12582912 | tf_op args[4]
  34.8 8.5 %fusion.179 = f32[1,64,1,1]{1,0,3,2:T(1,128)S(1)} fusion(bf16[16,8,384,1]{2,1,0,3:T(8,128)(2,1)S(1)} %convert_bitcast_fusion, bf16[64,16,8,384]{3,2,1,0:T(8,128)(2,1)} %param.9), kind=kOutput, calls=%fused_computation.312 | convolution fusion | flops 6291456 | bytes 6390016 | tf_op jit(solution)/shard_map/dot_general | solution.py:135
  43.3 6.3 %copy.373 = bf16[64,16,8,384]{3,0,1,2:T(8,128)(2,1)} copy(bf16[64,16,8,384]{3,2,1,0:T(8,128)(2,1)S(1)} %bitcast.718) | data formatting | bytes 12582912 | tf_op args[4]
  49.6 18.2 %copy.394 = bf16[8,8,128,384]{3,1,2,0:T(8,128)(2,1)} copy(bf16[8,8,128,384]{3,2,1,0:T(8,128)(2,1)S(1)} %bitcast.719) | data formatting | bytes 12582912
  68.8 15.9 %subtract_convert_fusion = bf16[64,16,8,384]{3,2,1,0:T(8,128)(2,1)S(1)} fusion(bf16[64,16,8,384]{3,2,1,0:T(8,128)(2,1)S(1)} %bitcast.718, f32[16,8,384]{2,1,0:T(8,128)S(1)} %get-tuple-element.28, f32[16,8,384]{2,1,0:T(8,128)S(1)} %get-tuple-element.27, f32[16,8,384]{2,1,0:T(8,128)S(1)} %get-tuple-element.26, f32[16,8,384]{2,1,0:T(8,128)S(1)} %get-tuple-element.25, ...), kind=kLoop, calls=%fused_computation.6 | loop fusion | flops 66060288 | bytes 13959168 | tf_op jit(solution)/shard_map/convert_element_type | solution.py:101
  84.7 15.4 %fusion.8 = f32[64,64]{1,0:T(8,128)S(1)} fusion(bf16[64,16,8,384]{3,2,1,0:T(8,128)(2,1)S(1)} %subtract_convert_fusion, bf16[64,16,8,384]{3,2,1,0:T(8,128)(2,1)S(1)} %bitcast.718), kind=kOutput, calls=%fused_computation.19 | convolution fusion | flops 402653184 | bytes 12599296 | tf_op jit(solution)/shard_map/dot_general | solution.py:102
  100.2 5.8 cholesky.17
  107.3 4.9 custom-call.6
  127.2 5.2 collective-permute-start.9
  138.8 8.5 %collective-permute-done.10 = bf16[64,18,1,384]{3,0,1,2:T(8,128)(2,1)S(1)} collective-permute-done((bf16[64,18,1,384]{3,0,1,2:T(8,128)(2,1)S(1)}, bf16[64,18,1,384]{3,0,1,2:T(8,128)(2,1)S(1)}, u32[]{:S(2)}, u32[]{:S(2)}) %collective-permute-start.10) | collective-permute-done | bytes 884768 | tf_op jit(solution)/shard_map/ppermute | solution.py:24
  147.7 7.5 %collective-permute-done.8 = bf16[64,18,1,384]{3,0,1,2:T(8,128)(2,1)S(1)} collective-permute-done((bf16[64,18,1,384]{3,0,1,2:T(8,128)(2,1)S(1)}, bf16[64,18,1,384]{3,0,1,2:T(8,128)(2,1)S(1)}, u32[]{:S(2)}, u32[]{:S(2)}) %collective-permute-start.8) | collective-permute-done | bytes 884768 | tf_op jit(solution)/shard_map/ppermute | solution.py:22
  171.7 4.9 collective-permute-start.16
  178.6 5.6 collective-permute-start.18
  186.4 5.0 collective-permute-start.20
  212.2 6.8 %collective-permute-start.26 = (f32[18,1,384]{2,1,0:T(1,128)S(1)}, f32[18,1,384]{2,1,0:T(1,128)S(1)}, u32[]{:S(2)}, u32[]{:S(2)}) collective-permute-start(f32[18,1,384]{2,1,0:T(1,128)S(1)} %get-tuple-element.41), channel_id=1, source_target_pairs={{0,1},{1,2},{2,3},{3,4},{4,5},{5,6},{6,7},{7,8},{8,9},{9,10},{10,1... | collective-permute-start | bytes 82952 | tf_op jit(solution)/shard_map/ppermute | solution.py:22
  219.7 9.1 %fusion.177 = f32[1,64,1,1]{1,0,3,2:T(1,128)S(1)} fusion(bf16[16,8,384,1]{2,1,0,3:T(8,128)(2,1)S(1)} %fusion.182, bf16[64,16,8,384]{3,2,1,0:T(8,128)(2,1)} %param.9), kind=kOutput, calls=%fused_computation.310 | convolution fusion | flops 6291456 | bytes 6390016 | tf_op jit(solution)/shard_map/dot_general | solution.py:135
  230.9 5.1 collective-permute-start.28
  238.0 6.6 %collective-permute-start.30 = (f32[3,1,64]{2,1,0:T(1,128)S(1)}, f32[3,1,64]{2,1,0:T(1,128)S(1)}, u32[]{:S(2)}, u32[]{:S(2)}) collective-permute-start(f32[3,1,64]{2,1,0:T(1,128)S(1)} %pad_maximum_fusion.65), channel_id=1, source_target_pairs={{0,1},{1,2},{2,3},{3,4},{4,5},{5,6},{6,7},{7,8},{8,9},{9,10},{10,1... | collective-permute-start | bytes 2312 | tf_op jit(solution)/shard_map/ppermute | solution.py:22
  247.8 5.0 collective-permute-start.32
  254.8 6.6 %collective-permute-start.34 = (f32[3,1,64]{2,1,0:T(1,128)S(1)}, f32[3,1,64]{2,1,0:T(1,128)S(1)}, u32[]{:S(2)}, u32[]{:S(2)}) collective-permute-start(f32[3,1,64]{2,1,0:T(1,128)S(1)} %pad_maximum_fusion.66), channel_id=1, source_target_pairs={{0,1},{1,2},{2,3},{3,4},{4,5},{5,6},{6,7},{7,8},{8,9},{9,10},{10,1... | collective-permute-start | bytes 2312 | tf_op jit(solution)/shard_map/ppermute | solution.py:22
  264.6 5.0 collective-permute-start.36
  271.6 6.5 %collective-permute-start.38 = (f32[3,1,64]{2,1,0:T(1,128)S(1)}, f32[3,1,64]{2,1,0:T(1,128)S(1)}, u32[]{:S(2)}, u32[]{:S(2)}) collective-permute-start(f32[3,1,64]{2,1,0:T(1,128)S(1)} %pad_maximum_fusion.67), channel_id=1, source_target_pairs={{0,1},{1,2},{2,3},{3,4},{4,5},{5,6},{6,7},{7,8},{8,9},{9,10},{10,1... | collective-permute-start | bytes 2312 | tf_op jit(solution)/shard_map/ppermute | solution.py:22
  285.9 5.0 collective-permute-start.40
  293.1 6.7 %collective-permute-start.42 = (f32[18,1,384]{2,1,0:T(1,128)S(1)}, f32[18,1,384]{2,1,0:T(1,128)S(1)}, u32[]{:S(2)}, u32[]{:S(2)}) collective-permute-start(f32[18,1,384]{2,1,0:T(1,128)S(1)} %get-tuple-element.39), channel_id=1, source_target_pairs={{0,1},{1,2},{2,3},{3,4},{4,5},{5,6},{6,7},{7,8},{8,9},{9,10},{10,1... | collective-permute-start | bytes 82952 | tf_op jit(solution)/shard_map/ppermute | solution.py:22
  302.3 78.7 %all-reduce.7 = (f32[]{:T(128)}, f32[]{:T(128)}) all-reduce(f32[]{:T(128)} %get-tuple-element.18, f32[]{:T(128)} %get-tuple-element.16), channel_id=1, replica_groups=mesh['row'=8,'col'=16] {'row','col'}, use_global_device_ids=true, to_apply=%region_4.5 | all-reduce | flops 2 | bytes 16 | tf_op jit(solution)/shard_map/psum | solution.py:161
  396.9 65.2 %psum.30 = f32[]{:T(128)} all-reduce(f32[]{:T(128)} %get-tuple-element.14), channel_id=1, replica_groups=mesh['row'=8,'col'=16] {'row','col'}, use_global_device_ids=true, to_apply=%region_8.9 | all-reduce | flops 1 | bytes 8 | tf_op jit(solution)/shard_map/psum | solution.py:167
  465.7 9.1 %fusion.175 = f32[1,64,1,1]{1,0,3,2:T(1,128)S(1)} fusion(bf16[16,8,384,1]{2,1,0,3:T(8,128)(2,1)S(1)} %fusion.181, bf16[64,16,8,384]{3,2,1,0:T(8,128)(2,1)} %param.9), kind=kOutput, calls=%fused_computation.308 | convolution fusion | flops 6291456 | bytes 6390016 | tf_op jit(solution)/shard_map/dot_general | solution.py:135
  504.8 5.0 collective-permute-start.56
  511.8 4.8 collective-permute-start.58
  524.1 5.0 collective-permute-start.60
  537.6 73.9 %psum.31 = f32[]{:T(128)} all-reduce(f32[]{:T(128)} %get-tuple-element.12), channel_id=1, replica_groups=mesh['row'=8,'col'=16] {'row','col'}, use_global_device_ids=true, to_apply=%region_10.11 | all-reduce | flops 1 | bytes 8 | tf_op jit(solution)/shard_map/psum | solution.py:164
  (306 shorter events, 181.4 us)
Async XLA Ops:
  2.0 27.6 %collective-permute-start = (f32[1,8,384]{2,1,0:T(8,128)S(1)}, f32[1,8,384]{2,1,0:T(8,128)S(1)}, u32[]{:S(2)}, u32[]{:S(2)}) collective-permute-start(f32[1,8,384]{2,1,0:T(8,128)S(1)} %copy.353), channel_id=1, source_target_pairs={{0,16},{16,32},{32,48},{48,64},{64,80},{80,96},{96,112},{1,17},{17... | collective-permute-start | bytes 36872 | tf_op jit(solution)/shard_map/ppermute | solution.py:22
  7.1 22.4 %collective-permute-start.1 = (f32[1,8,384]{2,1,0:T(8,128)S(1)}, f32[1,8,384]{2,1,0:T(8,128)S(1)}, u32[]{:S(2)}, u32[]{:S(2)}) collective-permute-start(f32[1,8,384]{2,1,0:T(8,128)S(1)} %copy.357), channel_id=1, source_target_pairs={{16,0},{32,16},{48,32},{64,48},{80,64},{96,80},{112,96},{17,1},{33... | collective-permute-start | bytes 36872 | tf_op jit(solution)/shard_map/ppermute | solution.py:24
  17.0 105.4 %collective-permute-start.6 = (bf16[64,1,8,384]{3,0,2,1:T(8,128)(2,1)}, bf16[64,1,8,384]{3,0,2,1:T(8,128)(2,1)}, u32[]{:S(2)}, u32[]{:S(2)}) collective-permute-start(bf16[64,1,8,384]{3,0,2,1:T(8,128)(2,1)} %get-tuple-element.34), channel_id=1, source_target_pairs={{16,0},{32,16},{48,32},{64,48},{80,64},{96,80},{112,96},{17,1},{33... | collective-permute-start | bytes 1179656 | tf_op jit(solution)/shard_map/ppermute | solution.py:24
  18.9 103.5 %collective-permute-start.4 = (bf16[64,1,8,384]{3,0,2,1:T(8,128)(2,1)}, bf16[64,1,8,384]{3,0,2,1:T(8,128)(2,1)}, u32[]{:S(2)}, u32[]{:S(2)}) collective-permute-start(bf16[64,1,8,384]{3,0,2,1:T(8,128)(2,1)} %get-tuple-element.33), channel_id=1, source_target_pairs={{0,16},{16,32},{32,48},{48,64},{64,80},{80,96},{96,112},{1,17},{17... | collective-permute-start | bytes 1179656 | tf_op jit(solution)/shard_map/ppermute | solution.py:22
  29.6 38.2 %collective-permute-start.2 = (f32[18,1,384]{2,1,0:T(1,128)S(1)}, f32[18,1,384]{2,1,0:T(1,128)S(1)}, u32[]{:S(2)}, u32[]{:S(2)}) collective-permute-start(f32[18,1,384]{2,1,0:T(1,128)S(1)} %get-tuple-element.46), channel_id=1, source_target_pairs={{0,1},{1,2},{2,3},{3,4},{4,5},{5,6},{6,7},{7,8},{8,9},{9,10},{10,1... | collective-permute-start | bytes 82952 | tf_op jit(solution)/shard_map/ppermute | solution.py:22
  32.8 35.0 %collective-permute-start.3 = (f32[18,1,384]{2,1,0:T(1,128)S(1)}, f32[18,1,384]{2,1,0:T(1,128)S(1)}, u32[]{:S(2)}, u32[]{:S(2)}) collective-permute-start(f32[18,1,384]{2,1,0:T(1,128)S(1)} %get-tuple-element.45), channel_id=1, source_target_pairs={{1,0},{2,1},{3,2},{4,3},{5,4},{6,5},{7,6},{8,7},{9,8},{10,9},{11,1... | collective-permute-start | bytes 82952 | tf_op jit(solution)/shard_map/ppermute | solution.py:24
  112.9 13.0 %collective-permute-start.7 = (f32[1,1,64]{2,1,0:T(1,128)S(1)}, f32[1,1,64]{2,1,0:T(1,128)S(1)}, u32[]{:S(2)}, u32[]{:S(2)}) collective-permute-start(f32[1,1,64]{2,1,0:T(1,128)S(1)} %bitcast.736), channel_id=1, source_target_pairs={{16,0},{32,16},{48,32},{64,48},{80,64},{96,80},{112,96},{17,1},{33... | collective-permute-start | bytes 776 | tf_op jit(solution)/shard_map/ppermute | solution.py:24
  114.8 11.1 %collective-permute-start.5 = (f32[1,1,64]{2,1,0:T(1,128)S(1)}, f32[1,1,64]{2,1,0:T(1,128)S(1)}, u32[]{:S(2)}, u32[]{:S(2)}) collective-permute-start(f32[1,1,64]{2,1,0:T(1,128)S(1)} %bitcast.737), channel_id=1, source_target_pairs={{0,16},{16,32},{32,48},{48,64},{64,80},{80,96},{96,112},{1,17},{17... | collective-permute-start | bytes 776 | tf_op jit(solution)/shard_map/ppermute | solution.py:22
  124.3 23.1 %collective-permute-start.10 = (bf16[64,18,1,384]{3,0,1,2:T(8,128)(2,1)S(1)}, bf16[64,18,1,384]{3,0,1,2:T(8,128)(2,1)S(1)}, u32[]{:S(2)}, u32[]{:S(2)}) collective-permute-start(bf16[64,18,1,384]{3,0,1,2:T(8,128)(2,1)S(1)} %get-tuple-element.30), channel_id=1, source_target_pairs={{1,0},{2,1},{3,2},{4,3},{5,4},{6,5},{7,6},{8,7},{9,8},{10,9},{11,1... | collective-permute-start | bytes 2654216 | tf_op jit(solution)/shard_map/ppermute | solution.py:24
  125.9 29.7 %collective-permute-start.11 = (f32[3,1,64]{2,1,0:T(1,128)S(1)}, f32[3,1,64]{2,1,0:T(1,128)S(1)}, u32[]{:S(2)}, u32[]{:S(2)}) collective-permute-start(f32[3,1,64]{2,1,0:T(1,128)S(1)} %pad_maximum_fusion.62), channel_id=1, source_target_pairs={{1,0},{2,1},{3,2},{4,3},{5,4},{6,5},{7,6},{8,7},{9,8},{10,9},{11,1... | collective-permute-start | bytes 2312 | tf_op jit(solution)/shard_map/ppermute | solution.py:24
  127.2 28.6 %collective-permute-start.9 = (f32[3,1,64]{2,1,0:T(1,128)S(1)}, f32[3,1,64]{2,1,0:T(1,128)S(1)}, u32[]{:S(2)}, u32[]{:S(2)}) collective-permute-start(f32[3,1,64]{2,1,0:T(1,128)S(1)} %pad_maximum_fusion.62), channel_id=1, source_target_pairs={{0,1},{1,2},{2,3},{3,4},{4,5},{5,6},{6,7},{7,8},{8,9},{9,10},{10,1... | collective-permute-start | bytes 2312 | tf_op jit(solution)/shard_map/ppermute | solution.py:22
  132.4 22.8 %collective-permute-start.8 = (bf16[64,18,1,384]{3,0,1,2:T(8,128)(2,1)S(1)}, bf16[64,18,1,384]{3,0,1,2:T(8,128)(2,1)S(1)}, u32[]{:S(2)}, u32[]{:S(2)}) collective-permute-start(bf16[64,18,1,384]{3,0,1,2:T(8,128)(2,1)S(1)} %get-tuple-element.29), channel_id=1, source_target_pairs={{0,1},{1,2},{2,3},{3,4},{4,5},{5,6},{6,7},{7,8},{8,9},{9,10},{10,1... | collective-permute-start | bytes 2654216 | tf_op jit(solution)/shard_map/ppermute | solution.py:22
  169.7 7.1 %collective-permute-start.17 = (f32[1,1,64]{2,1,0:T(1,128)S(1)}, f32[1,1,64]{2,1,0:T(1,128)S(1)}, u32[]{:S(2)}, u32[]{:S(2)}) collective-permute-start(f32[1,1,64]{2,1,0:T(1,128)S(1)} %bitcast.742), channel_id=1, source_target_pairs={{16,0},{32,16},{48,32},{64,48},{80,64},{96,80},{112,96},{17,1},{33... | collective-permute-start | bytes 776 | tf_op jit(solution)/shard_map/ppermute | solution.py:24
  177.3 7.1 %collective-permute-start.19 = (f32[3,1,64]{2,1,0:T(1,128)S(1)}, f32[3,1,64]{2,1,0:T(1,128)S(1)}, u32[]{:S(2)}, u32[]{:S(2)}) collective-permute-start(f32[3,1,64]{2,1,0:T(1,128)S(1)} %pad_maximum_fusion.64), channel_id=1, source_target_pairs={{1,0},{2,1},{3,2},{4,3},{5,4},{6,5},{7,6},{8,7},{9,8},{10,9},{11,1... | collective-permute-start | bytes 2312 | tf_op jit(solution)/shard_map/ppermute | solution.py:24
  210.9 8.1 %collective-permute-start.27 = (f32[18,1,384]{2,1,0:T(1,128)S(1)}, f32[18,1,384]{2,1,0:T(1,128)S(1)}, u32[]{:S(2)}, u32[]{:S(2)}) collective-permute-start(f32[18,1,384]{2,1,0:T(1,128)S(1)} %get-tuple-element.42), channel_id=1, source_target_pairs={{1,0},{2,1},{3,2},{4,3},{5,4},{6,5},{7,6},{8,7},{9,8},{10,9},{11,1... | collective-permute-start | bytes 82952 | tf_op jit(solution)/shard_map/ppermute | solution.py:24
  212.2 7.3 %collective-permute-start.26 = (f32[18,1,384]{2,1,0:T(1,128)S(1)}, f32[18,1,384]{2,1,0:T(1,128)S(1)}, u32[]{:S(2)}, u32[]{:S(2)}) collective-permute-start(f32[18,1,384]{2,1,0:T(1,128)S(1)} %get-tuple-element.41), channel_id=1, source_target_pairs={{0,1},{1,2},{2,3},{3,4},{4,5},{5,6},{6,7},{7,8},{8,9},{9,10},{10,1... | collective-permute-start | bytes 82952 | tf_op jit(solution)/shard_map/ppermute | solution.py:22
  229.0 7.2 %collective-permute-start.29 = (f32[1,1,64]{2,1,0:T(1,128)S(1)}, f32[1,1,64]{2,1,0:T(1,128)S(1)}, u32[]{:S(2)}, u32[]{:S(2)}) collective-permute-start(f32[1,1,64]{2,1,0:T(1,128)S(1)} %bitcast.757), channel_id=1, source_target_pairs={{16,0},{32,16},{48,32},{64,48},{80,64},{96,80},{112,96},{17,1},{33... | collective-permute-start | bytes 776 | tf_op jit(solution)/shard_map/ppermute | solution.py:24
  236.7 8.1 %collective-permute-start.31 = (f32[3,1,64]{2,1,0:T(1,128)S(1)}, f32[3,1,64]{2,1,0:T(1,128)S(1)}, u32[]{:S(2)}, u32[]{:S(2)}) collective-permute-start(f32[3,1,64]{2,1,0:T(1,128)S(1)} %pad_maximum_fusion.65), channel_id=1, source_target_pairs={{1,0},{2,1},{3,2},{4,3},{5,4},{6,5},{7,6},{8,7},{9,8},{10,9},{11,1... | collective-permute-start | bytes 2312 | tf_op jit(solution)/shard_map/ppermute | solution.py:24
  238.0 7.4 %collective-permute-start.30 = (f32[3,1,64]{2,1,0:T(1,128)S(1)}, f32[3,1,64]{2,1,0:T(1,128)S(1)}, u32[]{:S(2)}, u32[]{:S(2)}) collective-permute-start(f32[3,1,64]{2,1,0:T(1,128)S(1)} %pad_maximum_fusion.65), channel_id=1, source_target_pairs={{0,1},{1,2},{2,3},{3,4},{4,5},{5,6},{6,7},{7,8},{8,9},{9,10},{10,1... | collective-permute-start | bytes 2312 | tf_op jit(solution)/shard_map/ppermute | solution.py:22
  245.8 7.1 %collective-permute-start.33 = (f32[1,1,64]{2,1,0:T(1,128)S(1)}, f32[1,1,64]{2,1,0:T(1,128)S(1)}, u32[]{:S(2)}, u32[]{:S(2)}) collective-permute-start(f32[1,1,64]{2,1,0:T(1,128)S(1)} %bitcast.751), channel_id=1, source_target_pairs={{16,0},{32,16},{48,32},{64,48},{80,64},{96,80},{112,96},{17,1},{33... | collective-permute-start | bytes 776 | tf_op jit(solution)/shard_map/ppermute | solution.py:24
  253.5 8.1 %collective-permute-start.35 = (f32[3,1,64]{2,1,0:T(1,128)S(1)}, f32[3,1,64]{2,1,0:T(1,128)S(1)}, u32[]{:S(2)}, u32[]{:S(2)}) collective-permute-start(f32[3,1,64]{2,1,0:T(1,128)S(1)} %pad_maximum_fusion.66), channel_id=1, source_target_pairs={{1,0},{2,1},{3,2},{4,3},{5,4},{6,5},{7,6},{8,7},{9,8},{10,9},{11,1... | collective-permute-start | bytes 2312 | tf_op jit(solution)/shard_map/ppermute | solution.py:24
  254.8 7.4 %collective-permute-start.34 = (f32[3,1,64]{2,1,0:T(1,128)S(1)}, f32[3,1,64]{2,1,0:T(1,128)S(1)}, u32[]{:S(2)}, u32[]{:S(2)}) collective-permute-start(f32[3,1,64]{2,1,0:T(1,128)S(1)} %pad_maximum_fusion.66), channel_id=1, source_target_pairs={{0,1},{1,2},{2,3},{3,4},{4,5},{5,6},{6,7},{7,8},{8,9},{9,10},{10,1... | collective-permute-start | bytes 2312 | tf_op jit(solution)/shard_map/ppermute | solution.py:22
  262.7 7.1 %collective-permute-start.37 = (f32[1,1,64]{2,1,0:T(1,128)S(1)}, f32[1,1,64]{2,1,0:T(1,128)S(1)}, u32[]{:S(2)}, u32[]{:S(2)}) collective-permute-start(f32[1,1,64]{2,1,0:T(1,128)S(1)} %bitcast.745), channel_id=1, source_target_pairs={{16,0},{32,16},{48,32},{64,48},{80,64},{96,80},{112,96},{17,1},{33... | collective-permute-start | bytes 776 | tf_op jit(solution)/shard_map/ppermute | solution.py:24
  270.3 8.0 %collective-permute-start.39 = (f32[3,1,64]{2,1,0:T(1,128)S(1)}, f32[3,1,64]{2,1,0:T(1,128)S(1)}, u32[]{:S(2)}, u32[]{:S(2)}) collective-permute-start(f32[3,1,64]{2,1,0:T(1,128)S(1)} %pad_maximum_fusion.67), channel_id=1, source_target_pairs={{1,0},{2,1},{3,2},{4,3},{5,4},{6,5},{7,6},{8,7},{9,8},{10,9},{11,1... | collective-permute-start | bytes 2312 | tf_op jit(solution)/shard_map/ppermute | solution.py:24
  271.6 7.1 %collective-permute-start.38 = (f32[3,1,64]{2,1,0:T(1,128)S(1)}, f32[3,1,64]{2,1,0:T(1,128)S(1)}, u32[]{:S(2)}, u32[]{:S(2)}) collective-permute-start(f32[3,1,64]{2,1,0:T(1,128)S(1)} %pad_maximum_fusion.67), channel_id=1, source_target_pairs={{0,1},{1,2},{2,3},{3,4},{4,5},{5,6},{6,7},{7,8},{8,9},{9,10},{10,1... | collective-permute-start | bytes 2312 | tf_op jit(solution)/shard_map/ppermute | solution.py:22
  283.9 7.1 %collective-permute-start.41 = (f32[1,8,384]{2,1,0:T(8,128)S(1)}, f32[1,8,384]{2,1,0:T(8,128)S(1)}, u32[]{:S(2)}, u32[]{:S(2)}) collective-permute-start(f32[1,8,384]{2,1,0:T(8,128)S(1)} %get-tuple-element.52), channel_id=1, source_target_pairs={{16,0},{32,16},{48,32},{64,48},{80,64},{96,80},{112,96},{17,1},{33... | collective-permute-start | bytes 36872 | tf_op jit(solution)/shard_map/ppermute | solution.py:24
  291.8 8.0 %collective-permute-start.43 = (f32[18,1,384]{2,1,0:T(1,128)S(1)}, f32[18,1,384]{2,1,0:T(1,128)S(1)}, u32[]{:S(2)}, u32[]{:S(2)}) collective-permute-start(f32[18,1,384]{2,1,0:T(1,128)S(1)} %get-tuple-element.40), channel_id=1, source_target_pairs={{1,0},{2,1},{3,2},{4,3},{5,4},{6,5},{7,6},{8,7},{9,8},{10,9},{11,1... | collective-permute-start | bytes 82952 | tf_op jit(solution)/shard_map/ppermute | solution.py:24
  293.1 7.6 %collective-permute-start.42 = (f32[18,1,384]{2,1,0:T(1,128)S(1)}, f32[18,1,384]{2,1,0:T(1,128)S(1)}, u32[]{:S(2)}, u32[]{:S(2)}) collective-permute-start(f32[18,1,384]{2,1,0:T(1,128)S(1)} %get-tuple-element.39), channel_id=1, source_target_pairs={{0,1},{1,2},{2,3},{3,4},{4,5},{5,6},{6,7},{7,8},{8,9},{9,10},{10,1... | collective-permute-start | bytes 82952 | tf_op jit(solution)/shard_map/ppermute | solution.py:22
  391.0 72.5 %collective-permute-start.47 = (f32[18,1,384]{2,1,0:T(1,128)}, f32[18,1,384]{2,1,0:T(1,128)}, u32[]{:S(2)}, u32[]{:S(2)}) collective-permute-start(f32[18,1,384]{2,1,0:T(1,128)} %get-tuple-element.38), channel_id=1, source_target_pairs={{1,0},{2,1},{3,2},{4,3},{5,4},{6,5},{7,6},{8,7},{9,8},{10,9},{11,1... | collective-permute-start | bytes 82952 | tf_op jit(solution)/shard_map/ppermute | solution.py:24
  392.3 71.3 %collective-permute-start.46 = (f32[18,1,384]{2,1,0:T(1,128)}, f32[18,1,384]{2,1,0:T(1,128)}, u32[]{:S(2)}, u32[]{:S(2)}) collective-permute-start(f32[18,1,384]{2,1,0:T(1,128)} %get-tuple-element.37), channel_id=1, source_target_pairs={{0,1},{1,2},{2,3},{3,4},{4,5},{5,6},{6,7},{7,8},{8,9},{9,10},{10,1... | collective-permute-start | bytes 82952 | tf_op jit(solution)/shard_map/ppermute | solution.py:22
  487.8 7.4 %collective-permute-start.53 = (f32[1,1,64]{2,1,0:T(1,128)S(1)}, f32[1,1,64]{2,1,0:T(1,128)S(1)}, u32[]{:S(2)}, u32[]{:S(2)}) collective-permute-start(f32[1,1,64]{2,1,0:T(1,128)S(1)} %bitcast.754), channel_id=1, source_target_pairs={{16,0},{32,16},{48,32},{64,48},{80,64},{96,80},{112,96},{17,1},{33... | collective-permute-start | bytes 776 | tf_op jit(solution)/shard_map/ppermute | solution.py:24
  502.8 7.1 %collective-permute-start.57 = (f32[1,1,64]{2,1,0:T(1,128)S(1)}, f32[1,1,64]{2,1,0:T(1,128)S(1)}, u32[]{:S(2)}, u32[]{:S(2)}) collective-permute-start(f32[1,1,64]{2,1,0:T(1,128)S(1)} %bitcast.739), channel_id=1, source_target_pairs={{16,0},{32,16},{48,32},{64,48},{80,64},{96,80},{112,96},{17,1},{33... | collective-permute-start | bytes 776 | tf_op jit(solution)/shard_map/ppermute | solution.py:24
  (63 other events, 1864.7 us)
where the time goes:
time: 622 us; the launch traced here: 615 us
  blocking collectives  218 us (35%)
  starting transfers between devices  207 us (33%)
  matrix products  65.2 us (10%)
  other arithmetic  44.5 us (7%)
  local copies, waits for them, and re-layouts  41.2 us (7%)
  waiting for transfers between devices  32.8 us (5%)
    ppermute x32, starting transfers between devices, extended_2(): lax.ppermute(tail, axis, [(i, (i + 1) % count) for i in range(ends)])  151 us
    psum x1, blocking collectives, body(): norm_now = lax.psum(jnp.sum(residual * residual), ('row', 'col'))  78.7 us
    psum x1, blocking collectives, body(): alpha = norm_now / lax.psum(jnp.sum(direction * image), ('row', 'col'))  73.9 us
    psum x1, blocking collectives, body(): norm_next = lax.psum(jnp.sum(residual * residual), ('row', 'col'))  65.2 us
    ppermute x32, starting transfers between devices, extended_2(): lax.ppermute(head, axis, [((i + 1) % count, i) for i in range(ends)])  56.2 us
    unnamed x69, local copies, waits for them, and re-layouts  32.1 us
    dot_general x3, matrix products, project(): jnp.dot(basis_flat, field.astype(jnp.bfloat16).reshape(-1), preferred_ele...  26.7 us
    ppermute x32, waiting for transfers between devices, extended_2(): lax.ppermute(tail, axis, [(i, (i + 1) % count) for i in range(ends)])  21.2 us
  transfers between devices with their start and end apart: 64, of which 27 were waited for; matrix products, arithmetic and copies ran while one was open for 17% of the time, Pallas kernels for 0%

commit v1 on v0

v1 whole, which is shorter than its diff:
```python
import functools

import jax
import jax.numpy as jnp
from jax import lax
from jax.experimental import pallas as pl
from jax.experimental.pallas import tpu as pltpu
from jax.sharding import PartitionSpec as P

K = 64
CX = 16
CY = 8
NZ = 384
TILES = 96
CLASSES = 8
EX = CX + 4
EY = 16
Y0 = 4
REACH = 3
BLOCKS = 8
relax = 0.8
keep = 0.2
highest = lax.Precision.HIGHEST
f32 = jnp.float32
bf16 = jnp.bfloat16
VMEM = pl.BlockSpec(memory_space=pltpu.VMEM)
SMEM = pl.BlockSpec(memory_space=pltpu.SMEM)


def call(kernel, outs, args, scratch=(), smem=0, flops=1000000, limit=48):
    return pl.pallas_call(
        kernel,
        out_shape=[jax.ShapeDtypeStruct(s, d) for s, d in outs],
        in_specs=[SMEM] * smem + [VMEM] * (len(args) - smem),
        out_specs=[VMEM] * len(outs),
        scratch_shapes=list(scratch),
        cost_estimate=pl.CostEstimate(flops=flops, bytes_accessed=4000000, transcendentals=0),
        compiler_params=pltpu.CompilerParams(vmem_limit_bytes=limit << 20),
    )(*args)


def ring(x, axis, shift):
    count = lax.axis_size(axis)
    return lax.ppermute(x, axis, [(i, (i + shift) % count) for i in range(count)])


def gather(payload, axes=("row", "col")):
    count = lax.axis_size(axes)
    return lax.all_to_all(jnp.broadcast_to(payload, (count, payload.shape[-1])), axes, 0, 0)


def harmonic(a, b):
    return 2.0 * a * b / jnp.maximum(a + b, 1e-6)


def lookup(ids, table):
    tiles = jnp.zeros(ids.shape, f32)
    for label in range(CLASSES):
        tiles = jnp.where(ids == label, table[label], tiles)
    tile = lax.broadcasted_iota(jnp.int32, (TILES, NZ), 0)
    cell = lax.broadcasted_iota(jnp.int32, (TILES, NZ), 1)
    spread = jnp.where(lax.shift_right_logical(cell, 2) == tile, 1.0, 0.0)
    return jnp.dot(tiles, spread, precision=highest, preferred_element_type=f32)


def down(v):
    return pltpu.roll(v, v.shape[-2] - 1, v.ndim - 2)


def up(v):
    return pltpu.roll(v, 1, v.ndim - 2)


def fore(v):
    return pltpu.roll(v, NZ - 1, v.ndim - 1)


def back(v):
    return pltpu.roll(v, 1, v.ndim - 1)


def faces_kernel(w_ref, fx_ref, fy_ref):
    source = lax.broadcasted_iota(jnp.int32, (K * CY, K * CY), 1)
    target = lax.broadcasted_iota(jnp.int32, (K * CY, K * CY), 0)
    order = jnp.where(source == (target & (K - 1)) * CY + lax.shift_right_logical(target, 6), 1.0, 0.0).astype(bf16)
    for side, x in ((0, 0), (1, CX - 1)):
        slab = w_ref[:, x].reshape(K * CY, NZ)
        fx_ref[side] = (
            jnp.dot(order, slab, preferred_element_type=f32).astype(bf16).reshape(CY, K, NZ)
        )
    ends = jnp.concatenate([order[:K], order[(CY - 1) * K :]], axis=0)
    for x in range(CX):
        slab = w_ref[:, x].reshape(K * CY, NZ)
        both = jnp.dot(ends, slab, preferred_element_type=f32).astype(bf16)
        fy_ref[0, x] = both[:K]
        fy_ref[1, x] = both[K:]


def galerkin_kernel(table, w_ref, id_ref, s_ref, r_ref, g_ref, p_ref, coef, bs, acc, gp):
    width = 4
    row = lax.broadcasted_iota(jnp.int32, (CY, NZ), 0)
    lane = lax.broadcasted_iota(jnp.int32, (CY, NZ), 1)
    cells = lookup(id_ref[...].reshape(CX * CY, TILES), table).reshape(CX, CY, NZ)
    before = jnp.zeros((CY, NZ), f32)
    for x in range(CX):
        c = cells[x]
        fx = harmonic(c, cells[x + 1]) if x < CX - 1 else jnp.zeros_like(c)
        fy = jnp.where(row < CY - 1, harmonic(c, down(c)), 0.0)
        fz = jnp.where(lane < NZ - 1, harmonic(c, fore(c)), 0.0)
        coef[0, x] = 0.5 * (s_ref[x] + before + fx + up(fy) + fy + back(fz) + fz)
        coef[1, x] = fx
        coef[2, x] = fy
        coef[3, x] = fz
        before = fx
    acc[...] = jnp.zeros_like(acc)
    gp[...] = jnp.zeros_like(gp)

    def block(xb, _):
        for xi in range(width):
            x = xb * width + xi
            xn = jnp.minimum(x + 1, CX - 1)
            half = coef[0, x]
            fx = coef[1, x]
            fy = coef[2, x]
            fz = coef[3, x]
            v = r_ref[x].astype(bf16).astype(f32)
            for k in range(K):
                w = w_ref[k, x].astype(f32)
                b = half * w - fx * w_ref[k, xn].astype(f32) - fy * down(w) - fz * fore(w)
                bs[xi, k] = b.astype(bf16)
                q = w * v
                gp[k] += q[:, :128] + q[:, 128:256] + q[:, 256:]
        total = None
        for xi in range(width):
            part = lax.dot_general(
                w_ref[:, xb * width + xi].reshape(K * CY, NZ),
                bs[xi].reshape(K * CY, NZ),
                (((1,), (1,)), ((), ())),
                preferred_element_type=f32,
            )
            total = part if total is None else total + part
        acc[...] += total
        return 0

    lax.fori_loop(0, CX // width, block, 0)
    ri = lax.broadcasted_iota(jnp.int32, (K * CY, K * CY), 0) & (CY - 1)
    ci = lax.broadcasted_iota(jnp.int32, (K * CY, K * CY), 1) & (CY - 1)
    same = jnp.where(ri == ci, acc[...], 0.0)
    kr = lax.shift_right_logical(lax.broadcasted_iota(jnp.int32, (K * CY, K), 0), 3)
    pick = jnp.where(kr == lax.broadcasted_iota(jnp.int32, (K * CY, K), 1), 1.0, 0.0)
    side = jnp.dot(same, pick, precision=highest, preferred_element_type=f32)
    g = lax.dot_general(pick, side, (((0,), (0,)), ((), ())), precision=highest, preferred_element_type=f32)
    g_ref[...] = g + g.T
    p_ref[...] = jnp.broadcast_to(jnp.sum(jnp.sum(gp[...], axis=1), axis=1, keepdims=True), (K, 128))


def coef_kernel(
    where, table, id_ref, ixm, ixp, iym, iyp, s_ref, sxm, sxp, sym, syp, ofx, ofy, g_ref, p_ref,
    fx_ref, fy_ref, fz_ref, dg_ref, inv_ref, b_ref, cells, stor,
):
    r = where[0]
    c = where[1]
    inside = lambda cond: jnp.where(cond, 1.0, 0.0)
    cells[...] = jnp.zeros_like(cells)
    cells[2 : 2 + CX, Y0 : Y0 + CY] = lookup(id_ref[...].reshape(CX * CY, TILES), table).reshape(CX, CY, NZ)
    low = lookup(ixm[...].reshape(2 * CY, TILES), table).reshape(2, CY, NZ) * inside(r > 0)
    high = lookup(ixp[...].reshape(2 * CY, TILES), table).reshape(2, CY, NZ) * inside(r < where[2] - 1)
    cells[0:2, Y0 : Y0 + CY] = low
    cells[2 + CX :, Y0 : Y0 + CY] = high
    xs = lax.broadcasted_iota(jnp.int32, (EX, NZ), 0)
    ok = jnp.where(xs < 2, inside(r > 0), jnp.where(xs >= CX + 2, inside(r < where[2] - 1), 1.0))
    for j in range(2):
        cells[:, Y0 - 2 + j] = lookup(iym[j], table) * ok * inside(c > 0)
        cells[:, Y0 + CY + j] = lookup(iyp[j], table) * ok * inside(c < where[3] - 1)
    stor[...] = jnp.zeros_like(stor)
    stor[2 : 2 + CX, Y0 : Y0 + CY] = s_ref[...]
    stor[1, Y0 : Y0 + CY] = sxm[0]
    stor[2 + CX, Y0 : Y0 + CY] = sxp[0]
    stor[2 : 2 + CX, Y0 - 1] = sym[...]
    stor[2 : 2 + CX, Y0 + CY] = syp[...]
    lane = lax.broadcasted_iota(jnp.int32, (EY, NZ), 1)
    before = jnp.zeros((EY, NZ), f32)
    for x in range(EX):
        v = cells[x]
        fx = harmonic(v, cells[x + 1]) if x < EX - 1 else jnp.zeros_like(v)
        fy = harmonic(v, down(v))
        fz = jnp.where(lane < NZ - 1, harmonic(v, fore(v)), 0.0)
        dg_ref[x] = stor[x] + before + fx + up(fy) + fy + back(fz) + fz
        fx_ref[x] = fx
        fy_ref[x] = fy
        fz_ref[x] = fz
        before = fx

    total = jnp.zeros((K, K), f32)
    for side, x in ((0, 1), (1, CX + 1)):
        for y in range(CY):
            w = ofx[side, y]
            scaled = (w.astype(f32) * fx_ref[x, pl.ds(Y0 + y, 1)]).astype(bf16)
            total += lax.dot_general(scaled, w, (((1,), (1,)), ((), ())), preferred_element_type=f32)
    for side, y in ((0, Y0 - 1), (1, Y0 + CY - 1)):
        for x in range(CX):
            w = ofy[side, x]
            scaled = (w.astype(f32) * fy_ref[2 + x, pl.ds(y, 1)]).astype(bf16)
            total += lax.dot_general(scaled, w, (((1,), (1,)), ((), ())), preferred_element_type=f32)
    a = g_ref[...] + 0.5 * (total + total.T)

    sub = lax.broadcasted_iota(jnp.int32, (K, K), 0)
    lan = lax.broadcasted_iota(jnp.int32, (K, K), 1)
    lan1 = lax.broadcasted_iota(jnp.int32, (1, K), 1)
    for k in range(K):
        pivot = 1.0 / a[k : k + 1, k : k + 1]
        line = jnp.where(lan1 == k, pivot, a[k : k + 1, :] * pivot)
        a = jnp.where(sub == k, line, jnp.where(lan == k, 0.0, a) - a[:, k : k + 1] * line)
    inv_ref[...] = a
    b_ref[...] = relax * jnp.dot(a, p_ref[...], precision=highest, preferred_element_type=f32)


def couple_kernel(fx_ref, fy_ref, inv_ref, b_ref, ofx, ofy, nxm, nxp, nym, nyp, f_ref, m_ref):
    f_parts = []
    for side, x, other in ((0, 1, nxm), (1, CX + 1, nxp)):
        total = jnp.zeros((K, K), f32)
        for y in range(CY):
            scaled = (ofx[side, y].astype(f32) * fx_ref[x, pl.ds(Y0 + y, 1)]).astype(bf16)
            total += lax.dot_general(scaled, other[y], (((1,), (1,)), ((), ())), preferred_element_type=f32)
        f_parts.append(total)
    for side, y, other in ((0, Y0 - 1, nym), (1, Y0 + CY - 1, nyp)):
        total = jnp.zeros((K, K), f32)
        for x in range(CX):
            scaled = (ofy[side, x].astype(f32) * fy_ref[2 + x, pl.ds(y, 1)]).astype(bf16)
            total += lax.dot_general(scaled, other[x], (((1,), (1,)), ((), ())), preferred_element_type=f32)
        f_parts.append(total)
    inv = inv_ref[...]
    eye = jnp.where(
        lax.broadcasted_iota(jnp.int32, (K, K), 0) == lax.broadcasted_iota(jnp.int32, (K, K), 1), 1.0 + keep, 0.0
    )
    for n in range(4):
        minus = relax * jnp.dot(inv, f_parts[n], precision=highest, preferred_element_type=f32)
        f_ref[n] = minus
        spot = (0, 4, 1, 3)[n]
        m_ref[:, spot * K : spot * K + K] = minus
    m_ref[:, 2 * K : 3 * K] = eye
    m_ref[:, 5 * K : 6 * K] = jnp.zeros((K, K), f32)
    m_ref[:, 6 * K : 8 * K] = b_ref[...]


R1_BLOCKS = ((-1, 0), (0, -1), (0, 0), (0, 1), (1, 0))
R2_BLOCKS = tuple((a, b) for a in range(-2, 3) for b in range(-2, 3) if abs(a) + abs(b) <= 2)
NEIGHBOURS = ((-1, 0), (1, 0), (0, -1), (0, 1))


def spread_kernel(blocks, radius, base_blocks, f_ref, b_ref, own_ref, nxm, nxp, nym, nyp, out_ref, y_ref, held):
    others = (nxm, nxp, nym, nyp)
    wide = -(-len(blocks) // 2) * 2 * K
    held[...] = jnp.zeros_like(held)
    for n, (a0, b0) in enumerate(NEIGHBOURS):
        for i, (a, b) in enumerate(blocks):
            at = (b + b0 + REACH) * K
            held[n, a + a0 + REACH, :, at : at + K] = others[n][:, i * K : i * K + K]
    for i, (a, b) in enumerate(blocks):
        at = (b + REACH) * K
        held[4, a + REACH, :, at : at + K] = own_ref[:, i * K : i * K + K]
    for a in range(-radius, radius + 1):
        total = keep * held[4, a + REACH]
        for n in range(4):
            total += jnp.dot(f_ref[n], held[n, a + REACH], precision=highest, preferred_element_type=f32)
        if a == 0:
            lane = lax.broadcasted_iota(jnp.int32, (K, BLOCKS * K), 1)
            sub = lax.broadcasted_iota(jnp.int32, (K, BLOCKS * K), 0)
            total += jnp.where(lane == sub + REACH * K, 1.0, 0.0)
        held[5, a + REACH] = total
    y = b_ref[...] + keep * own_ref[:, wide : wide + 128]
    for n in range(4):
        y += jnp.dot(f_ref[n], others[n][:, wide : wide + 128], precision=highest, preferred_element_type=f32)
    if radius == REACH:
        out_ref[...] = held[5]
        y_ref[...] = y
    else:
        out = tuple((a, b) for a in range(-radius, radius + 1) for b in range(-radius, radius + 1) if abs(a) + abs(b) <= radius)
        for i, (a, b) in enumerate(out):
            at = (b + REACH) * K
            out_ref[:, i * K : i * K + K] = held[5, a + REACH, :, at : at + K]
        if len(out) % 2:
            out_ref[:, len(out) * K : len(out) * K + K] = jnp.zeros((K, K), f32)
        wide_out = -(-len(out) // 2) * 2 * K
        out_ref[:, wide_out : wide_out + 128] = y


def expand_into(w_ref, y_ref, store):
    width = 4
    step = 16

    def layers(xb, _):
        def some(kb, sums):
            for ki in range(step):
                k = kb * step + ki
                y = jnp.broadcast_to(y_ref[pl.ds(k, 1)], (CY, 128))
                y = jnp.concatenate([y] * (NZ // 128), axis=1)
                sums = tuple(
                    sums[i] + y * w_ref[k, xb * width + i].astype(f32) for i in range(width)
                )
            return sums

        sums = lax.fori_loop(0, K // step, some, tuple(jnp.zeros((CY, NZ), f32) for _ in range(width)))
        for i in range(width):
            store(xb * width + i, sums[i])
        return 0

    lax.fori_loop(0, CX // width, layers, 0)


def project_row(w_ref, v_ref, gp):
    half = CX // 2
    step = 8
    for h in range(2):
        values = [v_ref[h * half + i].astype(bf16).astype(f32) for i in range(half)]

        def some(kb, _, h=h, values=values):
            for ki in range(step):
                k = kb * step + ki
                total = values[0] * w_ref[k, h * half].astype(f32)
                for i in range(1, half):
                    total += values[i] * w_ref[k, h * half + i].astype(f32)
                part = total[:, :128] + total[:, 128:256] + total[:, 256:]
                if h == 0:
                    gp[k] = part
                else:
                    gp[k] += part
            return 0

        lax.fori_loop(0, K // step, some, 0)
    lanes = jnp.sum(gp[...], axis=1)
    return lax.dot_general(
        jnp.ones((8, 128), f32), lanes, (((1,), (1,)), ((), ())), precision=highest, preferred_element_type=f32
    )


def apply_layer(v, x, fx_ref, fy_ref, fz_ref, dg_ref):
    here = v[x]
    fy = fy_ref[x]
    fz = fz_ref[x]
    out = dg_ref[x] * here - fx_ref[x - 1] * v[x - 1] - fx_ref[x] * v[x + 1]
    return out - up(fy * here) - fy * down(here) - back(fz * here) - fz * fore(here)


def fill(ext, own, xm, xp, ym, yp):
    ext[...] = jnp.zeros_like(ext)
    deep = xm.shape[0]
    ext[2 : 2 + CX, Y0 : Y0 + CY] = own[...]
    ext[2 - deep : 2, Y0 : Y0 + CY] = xm[...]
    ext[2 + CX : 2 + CX + deep, Y0 : Y0 + CY] = xp[...]
    if deep == 2:
        for j in range(2):
            ext[:, Y0 - 2 + j] = ym[j]
            ext[:, Y0 + CY + j] = yp[j]
    else:
        ext[2 : 2 + CX, Y0 - 1] = ym[...]
        ext[2 : 2 + CX, Y0 + CY] = yp[...]


def solve_rows(where, got, r_ref, got_ref):
    got_ref[...] = got[:, :128]
    r = where[0]
    c = where[1]
    rows = where[2]
    cols = where[3]
    lane = lax.broadcasted_iota(jnp.int32, (1, 128), 1)
    total = jnp.zeros((K, 128), f32)
    for a in range(-REACH, REACH + 1):
        at = jnp.clip(r + a, 0, rows - 1) * cols
        for q in range(BLOCKS // 2):
            b = 2 * q - REACH
            if min(abs(b), abs(b + 1)) + abs(a) > REACH:
                continue
            first = got_ref[pl.ds(at + jnp.clip(c + b, 0, cols - 1), 1)]
            second = got_ref[pl.ds(at + jnp.clip(c + b + 1, 0, cols - 1), 1)]
            total += r_ref[a + REACH, :, q * 128 : q * 128 + 128] * jnp.where(lane < K, first, second)
    return jnp.sum(total, axis=1, keepdims=True)


def rounded(y):
    return jnp.broadcast_to(y, (K, 128)).astype(bf16).astype(f32)


def fold(parts):
    parts = parts[:, :128] + parts[:, 128:256] + parts[:, 256:]
    return jnp.sum(parts, axis=0, keepdims=True)


def first_kernel(f_ref, b_ref, y_in, nxm, nxp, nym, nyp, w_ref, x_ref, yb):
    y = b_ref[...] + keep * y_in[...]
    for n, other in enumerate((nxm, nxp, nym, nyp)):
        y += jnp.dot(f_ref[n], other[...], precision=highest, preferred_element_type=f32)
    yb[...] = y.astype(bf16).astype(f32)

    def store(x, v):
        x_ref[x] = v

    expand_into(w_ref, yb, store)


def residual_kernel(
    x_ref, xm, xp, ym, yp, rhs_ref, rxm, rxp, rym, ryp, fx_ref, fy_ref, fz_ref, dg_ref, inv_ref, w_ref,
    r_ref, pay_ref, ext, mid, field, gp,
):
    fill(ext, x_ref, xm, xp, ym, yp)
    fill(mid, rhs_ref, rxm, rxp, rym, ryp)
    for x in range(1, EX - 1):
        mid[x] = mid[x] - apply_layer(ext, x, fx_ref, fy_ref, fz_ref, dg_ref)
    r_ref[...] = mid[2 : 2 + CX, Y0 : Y0 + CY]
    for x in range(CX):
        field[x] = apply_layer(mid, x + 2, fx_ref, fy_ref, fz_ref, dg_ref)[Y0 : Y0 + CY]
    g = project_row(w_ref, field, gp)
    b = relax * jnp.dot(g, inv_ref[...], precision=highest, preferred_element_type=f32)
    pay_ref[...] = jnp.concatenate([b[:1], b[:1]], axis=1)


def direction_kernel(where, got_ref, rr_ref, w_ref, base_ref, d_ref, yb, lines):
    yb[...] = rounded(solve_rows(where, got_ref, rr_ref, lines))

    def store(x, v):
        d_ref[x] = base_ref[x] - v

    expand_into(w_ref, yb, store)


def image_kernel(
    d_ref, xm, xp, ym, yp, r_ref, fx_ref, fy_ref, fz_ref, dg_ref, inv_ref, w_ref,
    i_ref, pay_ref, ext, mid, field, gp,
):
    fill(ext, d_ref, xm, xp, ym, yp)
    for x in range(1, EX - 1):
        mid[x] = apply_layer(ext, x, fx_ref, fy_ref, fz_ref, dg_ref)
    mid[0] = jnp.zeros((EY, NZ), f32)
    mid[EX - 1] = jnp.zeros((EY, NZ), f32)
    i_ref[...] = mid[2 : 2 + CX, Y0 : Y0 + CY]
    rr = jnp.zeros((CY, NZ), f32)
    dw = jnp.zeros((CY, NZ), f32)
    for x in range(CX):
        field[x] = apply_layer(mid, x + 2, fx_ref, fy_ref, fz_ref, dg_ref)[Y0 : Y0 + CY]
        rr += r_ref[x] * r_ref[x]
        dw += d_ref[x] * i_ref[x]
    g = project_row(w_ref, field, gp)
    b = relax * jnp.dot(g, inv_ref[...], precision=highest, preferred_element_type=f32)
    pay_ref[:, :K] = b[:1]
    pay_ref[:, K : 2 * K] = b[:1]
    pay_ref[:, 128:256] = fold(rr)
    pay_ref[:, 256:384] = fold(dw)


def total_of(got_ref, at):
    return jnp.sum(jnp.sum(got_ref[:, at : at + 128], axis=0, keepdims=True), axis=1, keepdims=True)


def last_kernel(
    e_ref, xm, xp, ym, yp, got_ref, r_ref, d_ref, i_ref, fx_ref, fy_ref, fz_ref, dg_ref,
    r1_ref, z_ref, az_ref, pay_ref, ext,
):
    alpha = total_of(got_ref, 128) / total_of(got_ref, 256)
    fill(ext, e_ref, xm, xp, ym, yp)
    rr = jnp.zeros((CY, NZ), f32)
    zi = jnp.zeros((CY, NZ), f32)
    za = jnp.zeros((CY, NZ), f32)
    for x in range(CX):
        image = i_ref[x]
        az = image - alpha * apply_layer(ext, x + 2, fx_ref, fy_ref, fz_ref, dg_ref)[Y0 : Y0 + CY]
        z = d_ref[x] - alpha * e_ref[x]
        r1 = r_ref[x] - alpha * image
        r1_ref[x] = r1
        z_ref[x] = z
        az_ref[x] = az
        rr += r1 * r1
        zi += z * image
        za += z * az
    pay_ref[:, 0:128] = fold(rr)
    pay_ref[:, 128:256] = fold(zi)
    pay_ref[:, 256:384] = fold(za)


def finish_kernel(got_ref, fin_ref, x_ref, d_ref, i_ref, r1_ref, z_ref, az_ref, sol_ref, res_ref):
    rr0 = total_of(got_ref, 128)
    dw0 = total_of(got_ref, 256)
    rr1 = total_of(fin_ref, 0)
    zi = total_of(fin_ref, 128)
    za = total_of(fin_ref, 256)
    alpha0 = rr0 / dw0
    beta = rr1 / rr0
    alpha1 = rr1 / (beta * beta * dw0 + 2.0 * beta * zi + za)
    for x in range(CX):
        d = d_ref[x]
        sol_ref[x] = x_ref[x] + alpha0 * d + alpha1 * (beta * d + z_ref[x])
        res_ref[x] = r1_ref[x] - alpha1 * (beta * i_ref[x] + az_ref[x])


def lateral(x):
    return (ring(x, "row", 1), ring(x, "row", -1), ring(x, "col", 1), ring(x, "col", -1))


def halo_deep(field, last):
    xm = ring(field[CX - 2 :], "row", 1)
    xp = ring(field[:2], "row", -1)
    low = jnp.concatenate([xm[:, :2], field[:, :2], xp[:, :2]], axis=0).transpose(1, 0, 2)
    high = jnp.concatenate([xm[:, CY - 2 :], field[:, CY - 2 :], xp[:, CY - 2 :]], axis=0).transpose(1, 0, 2)
    return (xm, xp, ring(high, "col", 1), ring(low, "col", -1))


def halo_edge(field):
    return (
        ring(field[CX - 1 :], "row", 1),
        ring(field[:1], "row", -1),
        ring(field[:, CY - 1], "col", 1),
        ring(field[:, 0], "col", -1),
    )


def body(rhs, storage, class_id, table, basis):
    where = jnp.stack(
        [lax.axis_index("row"), lax.axis_index("col"), lax.axis_size("row"), lax.axis_size("col")]
    ).astype(jnp.int32)
    field = (CX, CY, NZ)
    wide = (EX, EY, NZ)
    vm = pltpu.VMEM

    ids = halo_deep(class_id, TILES)
    stor = halo_edge(storage)
    rhs_halo = halo_edge(rhs)
    ofx, ofy = call(faces_kernel, [((2, CY, K, NZ), bf16), ((2, CX, K, NZ), bf16)], (basis,))
    near = (ring(ofx[1], "row", 1), ring(ofx[0], "row", -1), ring(ofy[1], "col", 1), ring(ofy[0], "col", -1))
    gram, proj = call(
        galerkin_kernel,
        [((K, K), f32), ((K, 128), f32)],
        (table, basis, class_id, storage, rhs),
        [vm((4,) + field, f32), vm((4, K, CY, NZ), bf16), vm((K * CY, K * CY), f32), vm((K, 8, 128), f32)],
        smem=1,
        flops=20000000,
    )
    fx, fy, fz, dg, inv, b = call(
        coef_kernel,
        [(wide, f32)] * 4 + [((K, K), f32), ((K, 128), f32)],
        (where, table, class_id) + ids + (storage,) + stor + (ofx, ofy, gram, proj),
        [vm(wide, f32), vm(wide, f32)],
        smem=2,
    )
    coefs = (fx, fy, fz, dg)
    minus_f, m1 = call(
        couple_kernel, [((4, K, K), f32), ((K, 8 * K), f32)], (fx, fy, inv, b, ofx, ofy) + near
    )
    held = [vm((6, 2 * REACH + 1, K, BLOCKS * K), f32)]
    m2, _ = call(
        functools.partial(spread_kernel, R1_BLOCKS, 2, None),
        [((K, 16 * K), f32), ((8, 128), f32)],
        (minus_f, b, m1) + lateral(m1),
        held,
    )
    rows, y2 = call(
        functools.partial(spread_kernel, R2_BLOCKS, 3, None),
        [((2 * REACH + 1, K, BLOCKS * K), f32), ((K, 128), f32)],
        (minus_f, b, m2) + lateral(m2),
        held,
    )
    yb = [vm((K, 128), f32)]
    line = yb + [vm((lax.axis_size(("row", "col")), 128), f32)]
    (x0,) = call(first_kernel, [(field, f32)], (minus_f, b, y2) + lateral(y2) + (basis,), yb)
    work = [vm(wide, f32), vm(wide, f32), vm(field, f32), vm((K, 8, 128), f32)]
    r0, pay = call(
        residual_kernel,
        [(field, f32), ((1, 128), f32)],
        (x0,) + halo_deep(x0, NZ) + (rhs,) + rhs_halo + coefs + (inv, basis),
        work,
    )
    (d0,) = call(direction_kernel, [(field, f32)], (where, gather(pay), rows, basis, r0), line, smem=1)
    image, pay = call(
        image_kernel,
        [(field, f32), ((1, 384), f32)],
        (d0,) + halo_deep(d0, NZ) + (r0,) + coefs + (inv, basis),
        work,
    )
    got = gather(pay)
    (e0,) = call(direction_kernel, [(field, f32)], (where, got, rows, basis, image), line, smem=1)
    r1, z, az, pay = call(
        last_kernel,
        [(field, f32)] * 3 + [((1, 384), f32)],
        (e0,) + halo_edge(e0) + (got, r0, d0, image) + coefs,
        [vm(wide, f32)],
    )
    return tuple(
        call(finish_kernel, [(field, f32)] * 2, (got, gather(pay), x0, d0, image, r1, z, az))
    )


def solution(mesh):
    placed = (
        P("row", "col", None),
        P("row", "col", None),
        P("row", "col", None),
        P(),
        P(None, "row", "col", None),
    )
    return jax.shard_map(
        body,
        mesh=mesh,
        in_specs=placed,
        out_specs=(P("row", "col", None), P("row", "col", None)),
        check_vma=False,
    )
```

time: 622 us -> 238 us (0.38)
  blocking collectives: 218 us -> 53.5 us
  starting transfers between devices: 207 us -> 62.6 us
  matrix products: 65.2 us -> 0 us
  Pallas kernels: 0 us -> 61.6 us
  other arithmetic: 44.5 us -> 0.2 us
  local copies, waits for them, and re-layouts: 41.2 us -> 8.83 us
  waiting for transfers between devices: 32.8 us -> 49 us
    psum x3 -> x0, blocking collectives: 218 us -> none  [the longest x1 78.7 us: body(): norm_now = lax.psum(jnp.sum(residual * residual), ('row', 'col'))]
    ppermute x64 -> x40, starting transfers between devices: 207 us -> 62.6 us  [ring(): lax.ppermute(x, axis, [(i, (i + shift) % count) for i in range(count)])]
    dot_general x69 -> x0, matrix products: 64.9 us -> none  [the longest x3 26.7 us: project(): jnp.dot(basis_flat, field.astype(jnp.bfloat16).reshape(-1), preferred_ele...]
    pallas_call x0 -> x13, Pallas kernels: none -> 61.6 us  [call(): pl.pallas_call(kernel, out_shape=[jax.ShapeDtypeStruct(s, d) for s, d in...]
    all_to_all x0 -> x3, blocking collectives: none -> 53.5 us  [gather(): lax.all_to_all(jnp.broadcast_to(payload, (count, payload.shape[-1])), axe...]
    unnamed x69 -> x68, local copies, waits for them, and re-layouts: 32.1 us -> 4.62 us
    convert_element_type x4 -> x0, other arithmetic: 18.3 us -> none  [the longest x1 15.9 us: coarse_blocks(): applied = local_stencil(basis, faces, diagonal).astype(jnp.bfloat16)]
    ppermute x64 -> x40, waiting for transfers between devices: 32.8 us -> 49 us  [ring(): lax.ppermute(x, axis, [(i, (i + shift) % count) for i in range(count)])]
  transfers between devices with their start and end apart: 64 -> 40, of which waited for: 27 -> 14; matrix products, arithmetic and copies ran while one was open for 17% -> 1% of each run, Pallas kernels for 0% -> 14%
where the time goes in v1:
time: 238 us; the launch traced here: 237 us
  starting transfers between devices  62.6 us (26%)
  Pallas kernels  61.6 us (26%)
  blocking collectives  53.5 us (22%)
  waiting for transfers between devices  49 us (21%)
  local copies, waits for them, and re-layouts  8.83 us (4%)
    ppermute x40, starting transfers between devices, ring(): lax.ppermute(x, axis, [(i, (i + shift) % count) for i in range(count)])  62.6 us
    pallas_call x13, Pallas kernels, call(): pl.pallas_call(kernel, out_shape=[jax.ShapeDtypeStruct(s, d) for s, d in...  61.6 us
    all_to_all x3, blocking collectives, gather(): lax.all_to_all(jnp.broadcast_to(payload, (count, payload.shape[-1])), axe...  53.5 us
    ppermute x40, waiting for transfers between devices, ring(): lax.ppermute(x, axis, [(i, (i + shift) % count) for i in range(count)])  49 us
  transfers between devices with their start and end apart: 40, of which 14 were waited for; matrix products, arithmetic and copies ran while one was open for 1% of the time, Pallas kernels for 14%

profile of v1, /device:TPU:1, one launch (start us, length us, event | category | flops | bytes accessed | tf_op | source)
XLA Modules:
  0.0 236.9 jit_solution(18089369916881033617)
XLA Ops:
  1.4 3.0 %collective-permute-start = (s32[2,8,96]{2,0,1:T(2,128)S(1)}, s32[2,8,96]{2,0,1:T(2,128)S(1)}, u32[]{:S(2)}, u32[]{:S(2)}) collective-permute-start(s32[2,8,96]{2,0,1:T(2,128)S(1)} %copy.57), channel_id=1, source_target_pairs={{0,16},{16,32},{32,48},{48,64},{64,80},{80,96},{96,112},{112,0},{1... | collective-permute-start | bytes 18440 | tf_op jit(solution)/shard_map/ppermute | solution.py:44
  7.1 4.6 %shard_map.68 = (bf16[2,8,64,384]{3,2,1,0:T(8,128)(2,1)S(1)}, bf16[2,16,64,384]{3,2,1,0:T(8,128)(2,1)S(1)}) custom-call(bf16[64,16,8,384]{3,2,1,0:T(8,128)(2,1)} %w_ref.13), custom_call_target="tpu_custom_call" | custom-call | flops 1000000 | bytes 4000000 | tf_op jit(solution)/shard_map/pallas_call | solution.py:31
  14.7 5.0 %collective-permute-start.11 = (bf16[16,64,384]{2,1,0:T(8,128)(2,1)}, bf16[16,64,384]{2,1,0:T(8,128)(2,1)}, u32[]{:S(2)}, u32[]{:S(2)}) collective-permute-start(bf16[16,64,384]{2,1,0:T(8,128)(2,1)} %get-tuple-element.48), channel_id=1, source_target_pairs={{0,15},{1,0},{2,1},{3,2},{4,3},{5,4},{6,5},{7,6},{8,7},{9,8},{10,9... | collective-permute-start | bytes 2359304 | tf_op jit(solution)/shard_map/ppermute | solution.py:44
  21.7 17.9 %collective-permute-done.2.iym = s32[2,20,96]{2,1,0:T(8,128)S(1)} collective-permute-done((s32[2,20,96]{2,1,0:T(8,128)S(1)}, s32[2,20,96]{2,1,0:T(8,128)S(1)}, u32[]{:S(2)}, u32[]{:S(2)}) %collective-permute-start.2) | collective-permute-done | bytes 15392 | tf_op jit(solution)/shard_map/ppermute | solution.py:44
  39.7 3.0 %collective-permute-done.3.iyp = s32[2,20,96]{2,1,0:T(8,128)S(1)} collective-permute-done((s32[2,20,96]{2,1,0:T(8,128)S(1)}, s32[2,20,96]{2,1,0:T(8,128)S(1)}, u32[]{:S(2)}, u32[]{:S(2)}) %collective-permute-start.3) | collective-permute-done | bytes 15392 | tf_op jit(solution)/shard_map/ppermute | solution.py:44
  42.8 6.0 %collective-permute-done.6.sym = f32[16,384]{1,0:T(8,128)S(1)} collective-permute-done((f32[16,384]{1,0:T(8,128)S(1)}, f32[16,384]{1,0:T(8,128)S(1)}, u32[]{:S(2)}, u32[]{:S(2)}) %collective-permute-start.6) | collective-permute-done | bytes 24608 | tf_op jit(solution)/shard_map/ppermute | solution.py:44
  48.9 14.0 %shard_map.69 = (f32[64,64]{1,0:T(8,128)S(1)}, f32[64,128]{1,0:T(8,128)S(1)}) custom-call(f32[8]{0:T(128)S(1)} %copy-done.22, bf16[64,16,8,384]{3,2,1,0:T(8,128)(2,1)} %w_ref.13, s32[16,8,96]{2,1,0:T(8,128)S(1)} %copy-done.12, f32[16,8,384]{2,1,0:T(8,128)S(1)} %copy-done.9, f32[16,8,384]{2,1,0:T(8,128)S(1)} %copy-done.10), custom_call_target="tpu_custom_call" | custom-call | flops 20000000 | bytes 4000000 | tf_op jit(solution)/shard_map/pallas_call | solution.py:31
  65.1 9.2 %shard_map.70 = (f32[20,16,384]{2,1,0:T(8,128)S(1)}, f32[20,16,384]{2,1,0:T(8,128)S(1)}, f32[20,16,384]{2,1,0:T(8,128)S(1)}, f32[20,16,384]{2,1,0:T(8,128)S(1)},...) custom-call(s32[4]{0:T(128)S(1)} %pad_add_fusion.where, f32[8]{0:T(128)S(1)} %copy-done.23, s32[16,8,96]{2,1,0:T(8,128)S(1)} %copy-done.13, ...), custom_call_target="tpu_custom_call" | custom-call | flops 1000000 | bytes 4000000 | tf_op jit(solution)/shard_map/pallas_call | solution.py:31
  74.4 3.1 %shard_map.71 = (f32[4,64,64]{2,1,0:T(8,128)S(1)}, f32[64,512]{1,0:T(8,128)S(1)}) custom-call(f32[20,16,384]{2,1,0:T(8,128)S(1)} %get-tuple-element.29.fx_ref, f32[20,16,384]{2,1,0:T(8,128)S(1)} %get-tuple-element.30.fy_ref, f32[64,64]{1,0:T(8,128)S(1)} %get-tuple-element.31.inv_ref, f32[64,128]{1,0:T(8,128)S(1)} %get-tuple-element.32.b_ref, ...), custom_call_target="tpu_custom_call" | custom-call | flops 1000000 | bytes 4000000 | tf_op jit(solution)/shard_map/pallas_call | solution.py:31
  79.4 6.5 %collective-permute-start.13 = (f32[64,512]{1,0:T(8,128)S(1)}, f32[64,512]{1,0:T(8,128)S(1)}, u32[]{:S(2)}, u32[]{:S(2)}) collective-permute-start(f32[64,512]{1,0:T(8,128)S(1)} %get-tuple-element.34.own_ref), channel_id=1, source_target_pairs={{0,112},{16,0},{32,16},{48,32},{64,48},{80,64},{96,80},{112,96},{1... | collective-permute-start | bytes 393224 | tf_op jit(solution)/shard_map/ppermute | solution.py:44
  86.5 2.6 %collective-permute-done.13.nxp = f32[64,512]{1,0:T(8,128)S(1)} collective-permute-done((f32[64,512]{1,0:T(8,128)S(1)}, f32[64,512]{1,0:T(8,128)S(1)}, u32[]{:S(2)}, u32[]{:S(2)}) %collective-permute-start.13) | collective-permute-done | bytes 131104 | tf_op jit(solution)/shard_map/ppermute | solution.py:44
  91.5 3.1 %collective-permute-start.19 = (f32[64,1024]{1,0:T(8,128)S(1)}, f32[64,1024]{1,0:T(8,128)S(1)}, u32[]{:S(2)}, u32[]{:S(2)}) collective-permute-start(f32[64,1024]{1,0:T(8,128)S(1)} %get-tuple-element.35.own_ref), channel_id=1, source_target_pairs={{0,15},{1,0},{2,1},{3,2},{4,3},{5,4},{6,5},{7,6},{8,7},{9,8},{10,9... | collective-permute-start | bytes 786440 | tf_op jit(solution)/shard_map/ppermute | solution.py:44
  94.7 2.6 %collective-permute-start.17 = (f32[64,1024]{1,0:T(8,128)S(1)}, f32[64,1024]{1,0:T(8,128)S(1)}, u32[]{:S(2)}, u32[]{:S(2)}) collective-permute-start(f32[64,1024]{1,0:T(8,128)S(1)} %get-tuple-element.35.own_ref), channel_id=1, source_target_pairs={{0,112},{16,0},{32,16},{48,32},{64,48},{80,64},{96,80},{112,96},{1... | collective-permute-start | bytes 786440 | tf_op jit(solution)/shard_map/ppermute | solution.py:44
  98.0 5.2 %collective-permute-done.18.nym = f32[64,1024]{1,0:T(8,128)S(1)} collective-permute-done((f32[64,1024]{1,0:T(8,128)S(1)}, f32[64,1024]{1,0:T(8,128)S(1)}, u32[]{:S(2)}, u32[]{:S(2)}) %collective-permute-start.18) | collective-permute-done | bytes 262176 | tf_op jit(solution)/shard_map/ppermute | solution.py:44
  103.2 3.2 %shard_map.73 = (f32[7,64,512]{2,1,0:T(8,128)S(1)}, f32[64,128]{1,0:T(8,128)S(1)}) custom-call(f32[4,64,64]{2,1,0:T(8,128)S(1)} %get-tuple-element.33.f_ref, f32[64,128]{1,0:T(8,128)S(1)} %get-tuple-element.32.b_ref, f32[64,1024]{1,0:T(8,128)S(1)} %get-tuple-element.35.own_ref, f32[64,1024]{1,0:T(8,128)S(1)} %collective-permute-done.16.nxm, ...), custom_call_target="tpu_custom_call" | custom-call | flops 1000000 | bytes 4000000 | tf_op jit(solution)/shard_map/pallas_call | solution.py:31
  106.5 3.0 %collective-permute-start.23 = (f32[64,128]{1,0:T(8,128)S(1)}, f32[64,128]{1,0:T(8,128)S(1)}, u32[]{:S(2)}, u32[]{:S(2)}) collective-permute-start(f32[64,128]{1,0:T(8,128)S(1)} %get-tuple-element.36.y_in), channel_id=1, source_target_pairs={{0,15},{1,0},{2,1},{3,2},{4,3},{5,4},{6,5},{7,6},{8,7},{9,8},{10,9... | collective-permute-start | bytes 98312 | tf_op jit(solution)/shard_map/ppermute | solution.py:44
  109.4 3.5 %collective-permute-start.21 = (f32[64,128]{1,0:T(8,128)S(1)}, f32[64,128]{1,0:T(8,128)S(1)}, u32[]{:S(2)}, u32[]{:S(2)}) collective-permute-start(f32[64,128]{1,0:T(8,128)S(1)} %get-tuple-element.36.y_in), channel_id=1, source_target_pairs={{0,112},{16,0},{32,16},{48,32},{64,48},{80,64},{96,80},{112,96},{1... | collective-permute-start | bytes 98312 | tf_op jit(solution)/shard_map/ppermute | solution.py:44
  115.5 4.4 %shard_map.74.x_ref = f32[16,8,384]{2,1,0:T(8,128)S(1)} custom-call(f32[4,64,64]{2,1,0:T(8,128)S(1)} %get-tuple-element.33.f_ref, f32[64,128]{1,0:T(8,128)S(1)} %get-tuple-element.32.b_ref, f32[64,128]{1,0:T(8,128)S(1)} %get-tuple-element.36.y_in, f32[64,128]{1,0:T(8,128)S(1)} %collective-permute-done.20.nxm, f32[64,128]{1,0:T(8,128)S(1)} %collective-permute-done.21.nxp, ...), custom_call_target="tpu_custom_call" | custom-call | flops 1000000 | bytes 4000000 | tf_op jit(solution)/shard_map/pallas_call | solution.py:31
  119.9 3.5 %collective-permute-start.24 = (f32[2,8,384]{2,0,1:T(2,128)S(1)}, f32[2,8,384]{2,0,1:T(2,128)S(1)}, u32[]{:S(2)}, u32[]{:S(2)}) collective-permute-start(f32[2,8,384]{2,0,1:T(2,128)S(1)} %copy.63), channel_id=1, source_target_pairs={{0,16},{16,32},{32,48},{48,64},{64,80},{80,96},{96,112},{112,0},{1... | collective-permute-start | bytes 73736 | tf_op jit(solution)/shard_map/ppermute | solution.py:44
  126.9 4.8 %collective-permute-start.27 = (f32[2,20,384]{2,1,0:T(8,128)S(1)}, f32[2,20,384]{2,1,0:T(8,128)S(1)}, u32[]{:S(2)}, u32[]{:S(2)}) collective-permute-start(f32[2,20,384]{2,1,0:T(8,128)S(1)} %maximum_bitcast_fusion.1), channel_id=1, source_target_pairs={{0,15},{1,0},{2,1},{3,2},{4,3},{5,4},{6,5},{7,6},{8,7},{9,8},{10,9... | collective-permute-start | bytes 184328 | tf_op jit(solution)/shard_map/ppermute | solution.py:44
  131.8 4.8 %collective-permute-start.31 = (f32[16,384]{1,0:T(8,128)S(1)}, f32[16,384]{1,0:T(8,128)S(1)}, u32[]{:S(2)}, u32[]{:S(2)}) collective-permute-start(f32[16,384]{1,0:T(8,128)S(1)} %bitcast.57), channel_id=1, source_target_pairs={{0,15},{1,0},{2,1},{3,2},{4,3},{5,4},{6,5},{7,6},{8,7},{9,8},{10,9... | collective-permute-start | bytes 73736 | tf_op jit(solution)/shard_map/ppermute | solution.py:44
  137.7 3.1 %collective-permute-done.28.rxm = f32[1,8,384]{2,1,0:T(8,128)S(1)} collective-permute-done((f32[1,8,384]{2,1,0:T(8,128)S(1)}, f32[1,8,384]{2,1,0:T(8,128)S(1)}, u32[]{:S(2)}, u32[]{:S(2)}) %collective-permute-start.28) | collective-permute-done | bytes 12320 | tf_op jit(solution)/shard_map/ppermute | solution.py:44
  140.9 5.4 %shard_map.75 = (f32[16,8,384]{2,1,0:T(8,128)S(1)}, f32[1,128]{1,0:T(1,128)S(1)}) custom-call(f32[16,8,384]{2,1,0:T(8,128)S(1)} %shard_map.74.x_ref, f32[2,8,384]{2,1,0:T(8,128)S(1)} %copy.45.xm, f32[2,8,384]{2,1,0:T(8,128)S(1)} %copy.46.xp, f32[2,20,384]{2,1,0:T(8,128)S(1)} %collective-permute-done.26.ym, f32[2,20,384]{2,1,0:T(8,128)S(1)} %collective-permute-done.27.yp, ...), custom_call_target="tpu_custom_call" | custom-call | flops 1000000 | bytes 4000000 | tf_op jit(solution)/shard_map/pallas_call | solution.py:31
  146.3 17.1 %all_to_all.24 = f32[128,1,128]{2,1,0:T(1,128)S(1)} all-to-all(f32[128,1,128]{2,1,0:T(1,128)S(1)} %broadcast_in_dim.6), channel_id=1, replica_groups=mesh['row'=8,'col'=16] {'row','col'}, dimensions={0} | all-to-all | bytes 131072 | tf_op jit(solution)/shard_map/all_to_all | solution.py:49
  163.4 4.3 %shard_map.76.d_ref = f32[16,8,384]{2,1,0:T(8,128)S(1)} custom-call(s32[4]{0:T(128)S(1)} %pad_add_fusion.where, f32[128,128]{1,0:T(8,128)S(1)} %bitcast.52, f32[7,64,512]{2,1,0:T(8,128)S(1)} %get-tuple-element.40.rr_ref, bf16[64,16,8,384]{3,2,1,0:T(8,128)(2,1)} %w_ref.13, f32[16,8,384]{2,1,0:T(8,128)S(1)} %get-tuple-element.41.base_ref.r_ref), custom_call_target="tpu_custom_call" | custom-call | flops 1000000 | bytes 4000000 | tf_op jit(solution)/shard_map/pallas_call | solution.py:31
  170.1 2.7 %collective-permute-done.33 = f32[2,8,384]{2,0,1:T(2,128)S(1)} collective-permute-done((f32[2,8,384]{2,0,1:T(2,128)S(1)}, f32[2,8,384]{2,0,1:T(2,128)S(1)}, u32[]{:S(2)}, u32[]{:S(2)}) %collective-permute-start.33) | collective-permute-done | bytes 24608 | tf_op jit(solution)/shard_map/ppermute | solution.py:44
  173.2 4.8 %collective-permute-start.35 = (f32[2,20,384]{2,1,0:T(8,128)S(1)}, f32[2,20,384]{2,1,0:T(8,128)S(1)}, u32[]{:S(2)}, u32[]{:S(2)}) collective-permute-start(f32[2,20,384]{2,1,0:T(8,128)S(1)} %maximum_bitcast_fusion.3), channel_id=1, source_target_pairs={{0,15},{1,0},{2,1},{3,2},{4,3},{5,4},{6,5},{7,6},{8,7},{9,8},{10,9... | collective-permute-start | bytes 184328 | tf_op jit(solution)/shard_map/ppermute | solution.py:44
  179.4 5.3 %shard_map.77 = (f32[16,8,384]{2,1,0:T(8,128)S(1)}, f32[1,384]{1,0:T(1,128)S(1)}) custom-call(f32[16,8,384]{2,1,0:T(8,128)S(1)} %shard_map.76.d_ref, f32[2,8,384]{2,1,0:T(8,128)S(1)} %copy.51.xm, f32[2,8,384]{2,1,0:T(8,128)S(1)} %copy.52.xp, f32[2,20,384]{2,1,0:T(8,128)S(1)} %collective-permute-done.34.ym, f32[2,20,384]{2,1,0:T(8,128)S(1)} %collective-permute-done.35.yp, ...), custom_call_target="tpu_custom_call" | custom-call | flops 1000000 | bytes 4000000 | tf_op jit(solution)/shard_map/pallas_call | solution.py:31
  185.5 19.5 %all_to_all.25 = f32[128,1,384]{2,1,0:T(1,128)S(1)} all-to-all(f32[128,1,384]{2,1,0:T(1,128)S(1)} %broadcast_in_dim.7), channel_id=1, replica_groups=mesh['row'=8,'col'=16] {'row','col'}, dimensions={0} | all-to-all | bytes 393216 | tf_op jit(solution)/shard_map/all_to_all | solution.py:49
  206.0 4.4 %shard_map.78.e_ref = f32[16,8,384]{2,1,0:T(8,128)S(1)} custom-call(s32[4]{0:T(128)S(1)} %pad_add_fusion.where, f32[128,384]{1,0:T(8,128)S(1)} %bitcast.48, f32[7,64,512]{2,1,0:T(8,128)S(1)} %get-tuple-element.40.rr_ref, bf16[64,16,8,384]{3,2,1,0:T(8,128)(2,1)} %w_ref.13, f32[16,8,384]{2,1,0:T(8,128)S(1)} %copy-done.5), custom_call_target="tpu_custom_call" | custom-call | flops 1000000 | bytes 4000000 | tf_op jit(solution)/shard_map/pallas_call | solution.py:31
  210.9 4.4 %collective-permute-start.39 = (f32[16,384]{1,0:T(8,128)S(1)}, f32[16,384]{1,0:T(8,128)S(1)}, u32[]{:S(2)}, u32[]{:S(2)}) collective-permute-start(f32[16,384]{1,0:T(8,128)S(1)} %bitcast.54), channel_id=1, source_target_pairs={{0,15},{1,0},{2,1},{3,2},{4,3},{5,4},{6,5},{7,6},{8,7},{9,8},{10,9... | collective-permute-start | bytes 73736 | tf_op jit(solution)/shard_map/ppermute | solution.py:44
  219.1 16.9 %all_to_all.26 = f32[128,1,384]{2,1,0:T(1,128)S(1)} all-to-all(f32[128,1,384]{2,1,0:T(1,128)S(1)} %broadcast_in_dim.8), channel_id=1, replica_groups=mesh['row'=8,'col'=16] {'row','col'}, dimensions={0} | all-to-all | bytes 393216 | tf_op jit(solution)/shard_map/all_to_all | solution.py:49
  (170 shorter events, 34.8 us)
Async XLA Ops:
  1.4 13.3 %collective-permute-start = (s32[2,8,96]{2,0,1:T(2,128)S(1)}, s32[2,8,96]{2,0,1:T(2,128)S(1)}, u32[]{:S(2)}, u32[]{:S(2)}) collective-permute-start(s32[2,8,96]{2,0,1:T(2,128)S(1)} %copy.57), channel_id=1, source_target_pairs={{0,16},{16,32},{32,48},{48,64},{64,80},{80,96},{96,112},{112,0},{1... | collective-permute-start | bytes 18440 | tf_op jit(solution)/shard_map/ppermute | solution.py:44
  4.4 15.3 %collective-permute-start.1 = (s32[2,8,96]{2,0,1:T(2,128)S(1)}, s32[2,8,96]{2,0,1:T(2,128)S(1)}, u32[]{:S(2)}, u32[]{:S(2)}) collective-permute-start(s32[2,8,96]{2,0,1:T(2,128)S(1)} %copy.58), channel_id=1, source_target_pairs={{0,112},{16,0},{32,16},{48,32},{64,48},{80,64},{96,80},{112,96},{1... | collective-permute-start | bytes 18440 | tf_op jit(solution)/shard_map/ppermute | solution.py:44
  5.1 14.6 %collective-permute-start.5 = (f32[1,8,384]{2,1,0:T(8,128)S(1)}, f32[1,8,384]{2,1,0:T(8,128)S(1)}, u32[]{:S(2)}, u32[]{:S(2)}) collective-permute-start(f32[1,8,384]{2,1,0:T(8,128)S(1)} %get-tuple-element.70), channel_id=1, source_target_pairs={{0,112},{16,0},{32,16},{48,32},{64,48},{80,64},{96,80},{112,96},{1... | collective-permute-start | bytes 36872 | tf_op jit(solution)/shard_map/ppermute | solution.py:44
  7.1 14.0 %collective-permute-start.4 = (f32[1,8,384]{2,1,0:T(8,128)S(1)}, f32[1,8,384]{2,1,0:T(8,128)S(1)}, u32[]{:S(2)}, u32[]{:S(2)}) collective-permute-start(f32[1,8,384]{2,1,0:T(8,128)S(1)} %get-tuple-element.71), channel_id=1, source_target_pairs={{0,16},{16,32},{32,48},{48,64},{64,80},{80,96},{96,112},{112,0},{1... | collective-permute-start | bytes 36872 | tf_op jit(solution)/shard_map/ppermute | solution.py:44
  12.7 61.7 %collective-permute-start.9 = (bf16[8,64,384]{2,1,0:T(8,128)(2,1)}, bf16[8,64,384]{2,1,0:T(8,128)(2,1)}, u32[]{:S(2)}, u32[]{:S(2)}) collective-permute-start(bf16[8,64,384]{2,1,0:T(8,128)(2,1)} %get-tuple-element.50), channel_id=1, source_target_pairs={{0,112},{16,0},{32,16},{48,32},{64,48},{80,64},{96,80},{112,96},{1... | collective-permute-start | bytes 1179656 | tf_op jit(solution)/shard_map/ppermute | solution.py:44
  14.7 59.6 %collective-permute-start.11 = (bf16[16,64,384]{2,1,0:T(8,128)(2,1)}, bf16[16,64,384]{2,1,0:T(8,128)(2,1)}, u32[]{:S(2)}, u32[]{:S(2)}) collective-permute-start(bf16[16,64,384]{2,1,0:T(8,128)(2,1)} %get-tuple-element.48), channel_id=1, source_target_pairs={{0,15},{1,0},{2,1},{3,2},{4,3},{5,4},{6,5},{7,6},{8,7},{9,8},{10,9... | collective-permute-start | bytes 2359304 | tf_op jit(solution)/shard_map/ppermute | solution.py:44
  19.7 54.7 %collective-permute-start.10 = (bf16[16,64,384]{2,1,0:T(8,128)(2,1)}, bf16[16,64,384]{2,1,0:T(8,128)(2,1)}, u32[]{:S(2)}, u32[]{:S(2)}) collective-permute-start(bf16[16,64,384]{2,1,0:T(8,128)(2,1)} %get-tuple-element.49), channel_id=1, source_target_pairs={{0,1},{1,2},{2,3},{3,4},{4,5},{5,6},{6,7},{7,8},{8,9},{9,10},{10,1... | collective-permute-start | bytes 2359304 | tf_op jit(solution)/shard_map/ppermute | solution.py:44
  19.8 54.6 %collective-permute-start.8 = (bf16[8,64,384]{2,1,0:T(8,128)(2,1)}, bf16[8,64,384]{2,1,0:T(8,128)(2,1)}, u32[]{:S(2)}, u32[]{:S(2)}) collective-permute-start(bf16[8,64,384]{2,1,0:T(8,128)(2,1)} %get-tuple-element.51), channel_id=1, source_target_pairs={{0,16},{16,32},{32,48},{48,64},{64,80},{80,96},{96,112},{112,0},{1... | collective-permute-start | bytes 1179656 | tf_op jit(solution)/shard_map/ppermute | solution.py:44
  21.7 18.0 %collective-permute-start.2 = (s32[2,20,96]{2,1,0:T(8,128)S(1)}, s32[2,20,96]{2,1,0:T(8,128)S(1)}, u32[]{:S(2)}, u32[]{:S(2)}) collective-permute-start(s32[2,20,96]{2,1,0:T(8,128)S(1)} %add_bitcast_fusion), channel_id=1, source_target_pairs={{0,1},{1,2},{2,3},{3,4},{4,5},{5,6},{6,7},{7,8},{8,9},{9,10},{10,1... | collective-permute-start | bytes 46088 | tf_op jit(solution)/shard_map/ppermute | solution.py:44
  42.8 6.0 %collective-permute-start.6 = (f32[16,384]{1,0:T(8,128)S(1)}, f32[16,384]{1,0:T(8,128)S(1)}, u32[]{:S(2)}, u32[]{:S(2)}) collective-permute-start(f32[16,384]{1,0:T(8,128)S(1)} %bitcast.58), channel_id=1, source_target_pairs={{0,1},{1,2},{2,3},{3,4},{4,5},{5,6},{6,7},{7,8},{8,9},{9,10},{10,1... | collective-permute-start | bytes 73736 | tf_op jit(solution)/shard_map/ppermute | solution.py:44
  48.8 14.1 %collective-permute-start.7 = (f32[16,384]{1,0:T(8,128)S(1)}, f32[16,384]{1,0:T(8,128)S(1)}, u32[]{:S(2)}, u32[]{:S(2)}) collective-permute-start(f32[16,384]{1,0:T(8,128)S(1)} %bitcast.59), channel_id=1, source_target_pairs={{0,15},{1,0},{2,1},{3,2},{4,3},{5,4},{6,5},{7,6},{8,7},{9,8},{10,9... | collective-permute-start | bytes 73736 | tf_op jit(solution)/shard_map/ppermute | solution.py:44
  77.5 9.0 %collective-permute-start.15 = (f32[64,512]{1,0:T(8,128)S(1)}, f32[64,512]{1,0:T(8,128)S(1)}, u32[]{:S(2)}, u32[]{:S(2)}) collective-permute-start(f32[64,512]{1,0:T(8,128)S(1)} %get-tuple-element.34.own_ref), channel_id=1, source_target_pairs={{0,15},{1,0},{2,1},{3,2},{4,3},{5,4},{6,5},{7,6},{8,7},{9,8},{10,9... | collective-permute-start | bytes 393224 | tf_op jit(solution)/shard_map/ppermute | solution.py:44
  77.6 8.9 %collective-permute-start.14 = (f32[64,512]{1,0:T(8,128)S(1)}, f32[64,512]{1,0:T(8,128)S(1)}, u32[]{:S(2)}, u32[]{:S(2)}) collective-permute-start(f32[64,512]{1,0:T(8,128)S(1)} %get-tuple-element.34.own_ref), channel_id=1, source_target_pairs={{0,1},{1,2},{2,3},{3,4},{4,5},{5,6},{6,7},{7,8},{8,9},{9,10},{10,1... | collective-permute-start | bytes 393224 | tf_op jit(solution)/shard_map/ppermute | solution.py:44
  79.4 9.8 %collective-permute-start.13 = (f32[64,512]{1,0:T(8,128)S(1)}, f32[64,512]{1,0:T(8,128)S(1)}, u32[]{:S(2)}, u32[]{:S(2)}) collective-permute-start(f32[64,512]{1,0:T(8,128)S(1)} %get-tuple-element.34.own_ref), channel_id=1, source_target_pairs={{0,112},{16,0},{32,16},{48,32},{64,48},{80,64},{96,80},{112,96},{1... | collective-permute-start | bytes 393224 | tf_op jit(solution)/shard_map/ppermute | solution.py:44
  91.5 6.4 %collective-permute-start.19 = (f32[64,1024]{1,0:T(8,128)S(1)}, f32[64,1024]{1,0:T(8,128)S(1)}, u32[]{:S(2)}, u32[]{:S(2)}) collective-permute-start(f32[64,1024]{1,0:T(8,128)S(1)} %get-tuple-element.35.own_ref), channel_id=1, source_target_pairs={{0,15},{1,0},{2,1},{3,2},{4,3},{5,4},{6,5},{7,6},{8,7},{9,8},{10,9... | collective-permute-start | bytes 786440 | tf_op jit(solution)/shard_map/ppermute | solution.py:44
  94.7 8.5 %collective-permute-start.18 = (f32[64,1024]{1,0:T(8,128)S(1)}, f32[64,1024]{1,0:T(8,128)S(1)}, u32[]{:S(2)}, u32[]{:S(2)}) collective-permute-start(f32[64,1024]{1,0:T(8,128)S(1)} %get-tuple-element.35.own_ref), channel_id=1, source_target_pairs={{0,1},{1,2},{2,3},{3,4},{4,5},{5,6},{6,7},{7,8},{8,9},{9,10},{10,1... | collective-permute-start | bytes 786440 | tf_op jit(solution)/shard_map/ppermute | solution.py:44
  94.7 8.5 %collective-permute-start.17 = (f32[64,1024]{1,0:T(8,128)S(1)}, f32[64,1024]{1,0:T(8,128)S(1)}, u32[]{:S(2)}, u32[]{:S(2)}) collective-permute-start(f32[64,1024]{1,0:T(8,128)S(1)} %get-tuple-element.35.own_ref), channel_id=1, source_target_pairs={{0,112},{16,0},{32,16},{48,32},{64,48},{80,64},{96,80},{112,96},{1... | collective-permute-start | bytes 786440 | tf_op jit(solution)/shard_map/ppermute | solution.py:44
  97.3 5.9 %collective-permute-start.16 = (f32[64,1024]{1,0:T(8,128)S(1)}, f32[64,1024]{1,0:T(8,128)S(1)}, u32[]{:S(2)}, u32[]{:S(2)}) collective-permute-start(f32[64,1024]{1,0:T(8,128)S(1)} %get-tuple-element.35.own_ref), channel_id=1, source_target_pairs={{0,16},{16,32},{32,48},{48,64},{64,80},{80,96},{96,112},{112,0},{1... | collective-permute-start | bytes 786440 | tf_op jit(solution)/shard_map/ppermute | solution.py:44
  106.5 7.0 %collective-permute-start.23 = (f32[64,128]{1,0:T(8,128)S(1)}, f32[64,128]{1,0:T(8,128)S(1)}, u32[]{:S(2)}, u32[]{:S(2)}) collective-permute-start(f32[64,128]{1,0:T(8,128)S(1)} %get-tuple-element.36.y_in), channel_id=1, source_target_pairs={{0,15},{1,0},{2,1},{3,2},{4,3},{5,4},{6,5},{7,6},{8,7},{9,8},{10,9... | collective-permute-start | bytes 98312 | tf_op jit(solution)/shard_map/ppermute | solution.py:44
  109.4 6.1 %collective-permute-start.22 = (f32[64,128]{1,0:T(8,128)S(1)}, f32[64,128]{1,0:T(8,128)S(1)}, u32[]{:S(2)}, u32[]{:S(2)}) collective-permute-start(f32[64,128]{1,0:T(8,128)S(1)} %get-tuple-element.36.y_in), channel_id=1, source_target_pairs={{0,1},{1,2},{2,3},{3,4},{4,5},{5,6},{6,7},{7,8},{8,9},{9,10},{10,1... | collective-permute-start | bytes 98312 | tf_op jit(solution)/shard_map/ppermute | solution.py:44
  109.4 6.1 %collective-permute-start.21 = (f32[64,128]{1,0:T(8,128)S(1)}, f32[64,128]{1,0:T(8,128)S(1)}, u32[]{:S(2)}, u32[]{:S(2)}) collective-permute-start(f32[64,128]{1,0:T(8,128)S(1)} %get-tuple-element.36.y_in), channel_id=1, source_target_pairs={{0,112},{16,0},{32,16},{48,32},{64,48},{80,64},{96,80},{112,96},{1... | collective-permute-start | bytes 98312 | tf_op jit(solution)/shard_map/ppermute | solution.py:44
  113.4 23.2 %collective-permute-start.29 = (f32[1,8,384]{2,1,0:T(8,128)S(1)}, f32[1,8,384]{2,1,0:T(8,128)S(1)}, u32[]{:S(2)}, u32[]{:S(2)}) collective-permute-start(f32[1,8,384]{2,1,0:T(8,128)S(1)} %get-tuple-element.62), channel_id=1, source_target_pairs={{0,112},{16,0},{32,16},{48,32},{64,48},{80,64},{96,80},{112,96},{1... | collective-permute-start | bytes 36872 | tf_op jit(solution)/shard_map/ppermute | solution.py:44
  119.9 5.4 %collective-permute-start.24 = (f32[2,8,384]{2,0,1:T(2,128)S(1)}, f32[2,8,384]{2,0,1:T(2,128)S(1)}, u32[]{:S(2)}, u32[]{:S(2)}) collective-permute-start(f32[2,8,384]{2,0,1:T(2,128)S(1)} %copy.63), channel_id=1, source_target_pairs={{0,16},{16,32},{32,48},{48,64},{64,80},{80,96},{96,112},{112,0},{1... | collective-permute-start | bytes 73736 | tf_op jit(solution)/shard_map/ppermute | solution.py:44
  126.8 14.1 %collective-permute-start.26 = (f32[2,20,384]{2,1,0:T(8,128)S(1)}, f32[2,20,384]{2,1,0:T(8,128)S(1)}, u32[]{:S(2)}, u32[]{:S(2)}) collective-permute-start(f32[2,20,384]{2,1,0:T(8,128)S(1)} %maximum_bitcast_fusion), channel_id=1, source_target_pairs={{0,1},{1,2},{2,3},{3,4},{4,5},{5,6},{6,7},{7,8},{8,9},{9,10},{10,1... | collective-permute-start | bytes 184328 | tf_op jit(solution)/shard_map/ppermute | solution.py:44
  126.9 14.0 %collective-permute-start.27 = (f32[2,20,384]{2,1,0:T(8,128)S(1)}, f32[2,20,384]{2,1,0:T(8,128)S(1)}, u32[]{:S(2)}, u32[]{:S(2)}) collective-permute-start(f32[2,20,384]{2,1,0:T(8,128)S(1)} %maximum_bitcast_fusion.1), channel_id=1, source_target_pairs={{0,15},{1,0},{2,1},{3,2},{4,3},{5,4},{6,5},{7,6},{8,7},{9,8},{10,9... | collective-permute-start | bytes 184328 | tf_op jit(solution)/shard_map/ppermute | solution.py:44
  131.7 9.1 %collective-permute-start.30 = (f32[16,384]{1,0:T(8,128)S(1)}, f32[16,384]{1,0:T(8,128)S(1)}, u32[]{:S(2)}, u32[]{:S(2)}) collective-permute-start(f32[16,384]{1,0:T(8,128)S(1)} %bitcast.55), channel_id=1, source_target_pairs={{0,1},{1,2},{2,3},{3,4},{4,5},{5,6},{6,7},{7,8},{8,9},{9,10},{10,1... | collective-permute-start | bytes 73736 | tf_op jit(solution)/shard_map/ppermute | solution.py:44
  131.8 9.0 %collective-permute-start.31 = (f32[16,384]{1,0:T(8,128)S(1)}, f32[16,384]{1,0:T(8,128)S(1)}, u32[]{:S(2)}, u32[]{:S(2)}) collective-permute-start(f32[16,384]{1,0:T(8,128)S(1)} %bitcast.57), channel_id=1, source_target_pairs={{0,15},{1,0},{2,1},{3,2},{4,3},{5,4},{6,5},{7,6},{8,7},{9,8},{10,9... | collective-permute-start | bytes 73736 | tf_op jit(solution)/shard_map/ppermute | solution.py:44
  136.6 4.2 %collective-permute-start.28 = (f32[1,8,384]{2,1,0:T(8,128)S(1)}, f32[1,8,384]{2,1,0:T(8,128)S(1)}, u32[]{:S(2)}, u32[]{:S(2)}) collective-permute-start(f32[1,8,384]{2,1,0:T(8,128)S(1)} %get-tuple-element.63), channel_id=1, source_target_pairs={{0,16},{16,32},{32,48},{48,64},{64,80},{80,96},{96,112},{112,0},{1... | collective-permute-start | bytes 36872 | tf_op jit(solution)/shard_map/ppermute | solution.py:44
  172.8 6.6 %collective-permute-start.34 = (f32[2,20,384]{2,1,0:T(8,128)S(1)}, f32[2,20,384]{2,1,0:T(8,128)S(1)}, u32[]{:S(2)}, u32[]{:S(2)}) collective-permute-start(f32[2,20,384]{2,1,0:T(8,128)S(1)} %maximum_bitcast_fusion.2), channel_id=1, source_target_pairs={{0,1},{1,2},{2,3},{3,4},{4,5},{5,6},{6,7},{7,8},{8,9},{9,10},{10,1... | collective-permute-start | bytes 184328 | tf_op jit(solution)/shard_map/ppermute | solution.py:44
  173.2 6.2 %collective-permute-start.35 = (f32[2,20,384]{2,1,0:T(8,128)S(1)}, f32[2,20,384]{2,1,0:T(8,128)S(1)}, u32[]{:S(2)}, u32[]{:S(2)}) collective-permute-start(f32[2,20,384]{2,1,0:T(8,128)S(1)} %maximum_bitcast_fusion.3), channel_id=1, source_target_pairs={{0,15},{1,0},{2,1},{3,2},{4,3},{5,4},{6,5},{7,6},{8,7},{9,8},{10,9... | collective-permute-start | bytes 184328 | tf_op jit(solution)/shard_map/ppermute | solution.py:44
  210.4 8.0 %collective-permute-start.38 = (f32[16,384]{1,0:T(8,128)S(1)}, f32[16,384]{1,0:T(8,128)S(1)}, u32[]{:S(2)}, u32[]{:S(2)}) collective-permute-start(f32[16,384]{1,0:T(8,128)S(1)} %bitcast.56), channel_id=1, source_target_pairs={{0,1},{1,2},{2,3},{3,4},{4,5},{5,6},{6,7},{7,8},{8,9},{9,10},{10,1... | collective-permute-start | bytes 73736 | tf_op jit(solution)/shard_map/ppermute | solution.py:44
  210.9 7.6 %collective-permute-start.39 = (f32[16,384]{1,0:T(8,128)S(1)}, f32[16,384]{1,0:T(8,128)S(1)}, u32[]{:S(2)}, u32[]{:S(2)}) collective-permute-start(f32[16,384]{1,0:T(8,128)S(1)} %bitcast.54), channel_id=1, source_target_pairs={{0,15},{1,0},{2,1},{3,2},{4,3},{5,4},{6,5},{7,6},{8,7},{9,8},{10,9... | collective-permute-start | bytes 73736 | tf_op jit(solution)/shard_map/ppermute | solution.py:44
  (32 other events, 561.6 us)
